TPU v7x, 32 devices: a whole 2x2x4 slice. The times are simulated.
32 devices in a mesh: expert: 8 (over z, y), head: 4 (over x, core).
Axes of the slice: x: 2, y: 2, z: 4, core: 2. Of those that a mesh axis runs over, the one named last changes fastest.
Arguments:
- block_input: bfloat16 [25216, 768], P(('expert', 'head')), may hold values from -6 to 6
- output_grad: bfloat16 [25216, 768], P(('expert', 'head')), may hold values from -6 to 6
- routes: int32 [25216, 2], P(('expert', 'head')), may hold values from 0 to 7, all different within a row; in each aligned block of 788 rows (0 to 787, 788 to 1575, ...) at most 316 rows name the same one
- qkv_master: float32 [768, 2304], P(('expert', 'head')), may hold values from -0.21875 to 0.21875
- qkv_mean: float32 [768, 2304], P(('expert', 'head')), may hold values from -512 to 512
- qkv_square: float32 [768, 2304], P(('expert', 'head')), may hold values from 4538.88 to 36311.04
- proj_master: float32 [768, 768], P(('expert', 'head')), may hold values from -0.875 to 0.875
- proj_mean: float32 [768, 768], P(('expert', 'head')), may hold values from -160 to 160
- proj_square: float32 [768, 768], P(('expert', 'head')), may hold values from 322.7648 to 2521.6
- router_master: float32 [768, 8], P(('expert', 'head')), may hold values from -0.109375 to 0.109375
- router_mean: float32 [768, 8], P(('expert', 'head')), may hold values from -4096 to 4096
- router_square: float32 [768, 8], P(('expert', 'head')), may hold values from 217866.23 to 1742929.9
- norm_master: float32 [4, 768], P(None, ('expert', 'head')), may hold values from -0.6 to 1.6
- norm_mean: float32 [4, 768], P(None, ('expert', 'head')), may hold values from -640 to 640
- norm_square: float32 [4, 768], P(None, ('expert', 'head')), may hold values from 6304 to 50432
- inner_master: float32 [8, 768, 3072], P('expert', None, 'head'), may hold values from -0.21875 to 0.21875
- inner_mean: float32 [8, 768, 3072], P('expert', None, 'head'), may hold values from -64 to 64
- inner_square: float32 [8, 768, 3072], P('expert', None, 'head'), may hold values from 70.92 to 567.36
- outer_master: float32 [8, 3072, 768], P('expert', 'head'), may hold values from -0.4375 to 0.4375
- outer_mean: float32 [8, 3072, 768], P('expert', 'head'), may hold values from -32 to 32
- outer_square: float32 [8, 3072, 768], P('expert', 'head'), may hold values from 17.73 to 141.84
Outputs:
- block_output: bfloat16 [25216, 768], P(('expert', 'head'))
- input_grad: float32 [25216, 768], P(('expert', 'head'))
- qkv_weight: float32 [768, 2304], P(('expert', 'head'))
- qkv_momentum: float32 [768, 2304], P(('expert', 'head'))
- qkv_variance: float32 [768, 2304], P(('expert', 'head'))
- qkv_copy: bfloat16 [768, 2304], P(('expert', 'head'))
- proj_weight: float32 [768, 768], P(('expert', 'head'))
- proj_momentum: float32 [768, 768], P(('expert', 'head'))
- proj_variance: float32 [768, 768], P(('expert', 'head'))
- proj_copy: bfloat16 [768, 768], P(('expert', 'head'))
- router_weight: float32 [768, 8], P(('expert', 'head'))
- router_momentum: float32 [768, 8], P(('expert', 'head'))
- router_variance: float32 [768, 8], P(('expert', 'head'))
- router_copy: bfloat16 [768, 8], P(('expert', 'head'))
- norm_weight: float32 [4, 768], P(None, ('expert', 'head'))
- norm_momentum: float32 [4, 768], P(None, ('expert', 'head'))
- norm_variance: float32 [4, 768], P(None, ('expert', 'head'))
- norm_copy: bfloat16 [4, 768], P(None, ('expert', 'head'))
- inner_weight: float32 [8, 768, 3072], P('expert', None, 'head')
- inner_momentum: float32 [8, 768, 3072], P('expert', None, 'head')
- inner_variance: float32 [8, 768, 3072], P('expert', None, 'head')
- inner_copy: bfloat16 [8, 768, 3072], P('expert', None, 'head')
- outer_weight: float32 [8, 3072, 768], P('expert', 'head')
- outer_momentum: float32 [8, 3072, 768], P('expert', 'head')
- outer_variance: float32 [8, 3072, 768], P('expert', 'head')
- outer_copy: bfloat16 [8, 3072, 768], P('expert', 'head')
Inputs may be any that keep to these rules, and one draw needn't show every extreme that they name: `routes`: in the rows of one device (aligned blocks of 788 rows) no expert is named more than 316 times, a bound that some block reaches; a row names two different experts.
All inputs are finite; a program needn't handle non-finite values.
Results may differ from a plain program's by a relative error of at most 0.017.
Values may be sent and summed in bfloat16 or wider, within the bound.
A program may use at most 320 MiB of HBM per device.

v0:
```python
import jax
import jax.numpy as jnp
from jax import lax
from jax.sharding import PartitionSpec as P

HD = 64
FF = 3072
SEQ = 197
STEP = 3


EPS_NORM = 1e-06
BETA_ONE = 0.5
BETA_TWO = 0.5
EPS_ADAM = 1e-08
DECAY = 0.1
NORM_RATE = 0.3


def layer_norm(values, gain_row, shift_row):
    centered = values - jnp.mean(values, axis=-1, keepdims=True)
    spread = lax.rsqrt(jnp.mean(centered * centered, axis=-1, keepdims=True) + EPS_NORM)
    return centered * spread * gain_row + shift_row


def gelu_tanh(values):
    return jax.nn.gelu(values, approximate=True)


def adam_step(master, first_state, square, gradient, step_rate):
    momentum = BETA_ONE * first_state + (1.0 - BETA_ONE) * gradient
    variance = BETA_TWO * square + (1.0 - BETA_TWO) * gradient * gradient
    first_fix = momentum / (1.0 - BETA_ONE**STEP)
    second_fix = variance / (1.0 - BETA_TWO**STEP)
    updated = master - step_rate * (first_fix / (jnp.sqrt(second_fix) + EPS_ADAM) + DECAY * master)
    return (updated, momentum, variance, updated.astype(jnp.bfloat16))


def slot_table(routes, expert_count, capacity):
    pair_expert = routes.reshape(-1)
    pair_count = pair_expert.shape[0]
    onehot = (pair_expert[:, None] == jnp.arange(expert_count, dtype=jnp.int32)[None, :]).astype(
        jnp.int32
    )
    before = jnp.cumsum(onehot, axis=0) - onehot
    position = jnp.sum(before * onehot, axis=1)
    target = pair_expert * capacity + position
    source = jnp.full((expert_count * capacity,), pair_count // 2, jnp.int32)
    source = source.at[target].set(jnp.arange(pair_count, dtype=jnp.int32) // 2)
    return (target, source)


def attention_weights(query_rows, key_rows, log_total, score_scale):
    scores = (
        jnp.einsum("bqhd,bkhd->bhqk", query_rows, key_rows, preferred_element_type=jnp.float32)
        * score_scale
    )
    return jnp.exp(scores - log_total)


def on_device(
    block_input,
    output_grad,
    routes,
    qkv_master,
    qkv_mean,
    qkv_square,
    proj_master,
    proj_mean,
    proj_square,
    router_master,
    router_mean,
    router_square,
    norm_master,
    norm_mean,
    norm_square,
    inner_master,
    inner_mean,
    inner_square,
    outer_master,
    outer_mean,
    outer_square,
):
    row_count = block_input.shape[0]
    model_width = block_input.shape[1]
    head_count = model_width // HD
    image_count = row_count // SEQ
    expert_count = router_master.shape[1]
    capacity = row_count * 16 // (5 * expert_count) + 1
    score_scale = HD ** (-0.5)
    qkv_full, proj_full, router_full, norm_full = (
        lax.all_gather(qkv_master.astype(jnp.bfloat16), ("expert", "head"), axis=0, tiled=True),
        lax.all_gather(proj_master.astype(jnp.bfloat16), ("expert", "head"), axis=0, tiled=True),
        lax.all_gather(router_master.astype(jnp.bfloat16), ("expert", "head"), axis=0, tiled=True),
        lax.all_gather(norm_master.astype(jnp.bfloat16), ("expert", "head"), axis=1, tiled=True),
    )
    inputs = block_input.astype(jnp.float32)
    norm_values = norm_full.astype(jnp.float32)
    normed, first_pull = jax.vjp(layer_norm, inputs, norm_values[0], norm_values[1])
    first_low = normed.astype(jnp.bfloat16)
    qkv_rows = jnp.dot(first_low, qkv_full, preferred_element_type=jnp.float32).astype(jnp.bfloat16)
    qkv_rows = qkv_rows.reshape(image_count, SEQ, head_count, 3, HD)
    query_rows = qkv_rows[:, :, :, 0]
    key_rows = qkv_rows[:, :, :, 1]
    value_rows = qkv_rows[:, :, :, 2]
    scores = (
        jnp.einsum("bqhd,bkhd->bhqk", query_rows, key_rows, preferred_element_type=jnp.float32)
        * score_scale
    )
    row_max = jnp.max(scores, axis=-1, keepdims=True)
    log_total = row_max + jnp.log(jnp.sum(jnp.exp(scores - row_max), axis=-1, keepdims=True))
    probs_low = jnp.exp(scores - log_total).astype(jnp.bfloat16)
    attended = jnp.einsum(
        "bhqk,bkhd->bqhd", probs_low, value_rows, preferred_element_type=jnp.float32
    )
    attended = attended.astype(jnp.bfloat16).reshape(row_count, model_width)
    middle = inputs + jnp.dot(attended, proj_full, preferred_element_type=jnp.float32)
    second, second_pull = jax.vjp(layer_norm, middle, norm_values[2], norm_values[3])
    second_low = second.astype(jnp.bfloat16)
    logits = jnp.dot(second_low, router_full, preferred_element_type=jnp.float32)
    choose = (
        routes[:, :, None] == jnp.arange(expert_count, dtype=jnp.int32)[None, None, :]
    ).astype(jnp.float32)

    def gate_of(logit_rows):
        return jnp.sum(jax.nn.softmax(logit_rows, axis=-1)[:, None, :] * choose, axis=-1)

    gate_values, gate_pull = jax.vjp(gate_of, logits)
    target, source = slot_table(routes, expert_count, capacity)
    padded = jnp.concatenate([second_low, jnp.zeros((1, model_width), jnp.bfloat16)], axis=0)
    outgoing = jnp.take(padded, source, axis=0).reshape(expert_count, capacity, model_width)
    arrived = lax.all_to_all(outgoing, "expert", split_axis=0, concat_axis=0, tiled=True)
    inner_low = inner_master.astype(jnp.bfloat16)[0]
    outer_low = outer_master.astype(jnp.bfloat16)[0]
    gathered = lax.all_gather(arrived, "head", axis=0, tiled=True).reshape(-1, model_width)
    hidden = jnp.dot(gathered, inner_low, preferred_element_type=jnp.float32)
    active, gelu_pull = jax.vjp(gelu_tanh, hidden)
    active_low = active.astype(jnp.bfloat16)
    partial_value = jnp.dot(active_low, outer_low, preferred_element_type=jnp.float32).reshape(
        -1, capacity, model_width
    )
    returned = lax.psum_scatter(
        partial_value.astype(jnp.bfloat16), "head", scatter_dimension=0, tiled=True
    )
    coming = lax.all_to_all(returned, "expert", split_axis=0, concat_axis=0, tiled=True)
    picked = (
        jnp.take(coming.reshape(-1, model_width), target, axis=0)
        .reshape(row_count, 2, model_width)
        .astype(jnp.float32)
    )
    block_output = (middle + jnp.sum(gate_values[:, :, None] * picked, axis=1)).astype(jnp.bfloat16)
    upstream = output_grad.astype(jnp.float32)
    gate_grad = jnp.sum(upstream[:, None, :] * picked, axis=-1)
    slot_rows = (
        (gate_values[:, :, None] * upstream[:, None, :])
        .astype(jnp.bfloat16)
        .reshape(-1, model_width)
    )
    slot_grads = (
        jnp.zeros((expert_count * capacity, model_width), jnp.bfloat16).at[target].set(slot_rows)
    )
    owner_grads = lax.all_to_all(
        slot_grads.reshape(expert_count, capacity, model_width),
        "expert",
        split_axis=0,
        concat_axis=0,
        tiled=True,
    )
    gathered_grads = lax.all_gather(owner_grads, "head", axis=0, tiled=True).reshape(
        -1, model_width
    )
    active_grad = jnp.einsum(
        "rd,fd->rf", gathered_grads, outer_low, preferred_element_type=jnp.float32
    )
    hidden_grad = gelu_pull(active_grad)[0].astype(jnp.bfloat16)
    outer_grad = jnp.einsum(
        "rf,rd->fd", active_low, gathered_grads, preferred_element_type=jnp.float32
    )[None]
    inner_grad = jnp.einsum("rd,rf->df", gathered, hidden_grad, preferred_element_type=jnp.float32)[
        None
    ]
    row_partial = jnp.einsum(
        "rf,df->rd", hidden_grad, inner_low, preferred_element_type=jnp.float32
    ).reshape(-1, capacity, model_width)
    row_grads = lax.psum_scatter(
        row_partial.astype(jnp.bfloat16), "head", scatter_dimension=0, tiled=True
    )
    back_rows = lax.all_to_all(row_grads, "expert", split_axis=0, concat_axis=0, tiled=True)
    pair_grads = (
        jnp.take(back_rows.reshape(-1, model_width), target, axis=0)
        .reshape(row_count, 2, model_width)
        .astype(jnp.float32)
    )
    logit_low = gate_pull(gate_grad)[0].astype(jnp.bfloat16)
    router_grad = jnp.einsum("td,te->de", second_low, logit_low, preferred_element_type=jnp.float32)
    second_grad = jnp.einsum(
        "te,de->td", logit_low, router_full, preferred_element_type=jnp.float32
    ) + jnp.sum(pair_grads, axis=1)
    middle_part, gain_two, shift_two = second_pull(second_grad)
    middle_grad = upstream + middle_part
    proj_input = middle_grad.astype(jnp.bfloat16)
    proj_grad = jnp.einsum("td,te->de", attended, proj_input, preferred_element_type=jnp.float32)
    attended_grad = jnp.einsum(
        "te,de->td", proj_input, proj_full, preferred_element_type=jnp.float32
    )
    attended_grad = attended_grad.astype(jnp.bfloat16).reshape(image_count, SEQ, head_count, HD)
    prob_rows = attention_weights(query_rows, key_rows, log_total, score_scale)
    probs_again = prob_rows.astype(jnp.bfloat16)
    value_grad = jnp.einsum(
        "bhqk,bqhd->bkhd", probs_again, attended_grad, preferred_element_type=jnp.float32
    )
    prob_grad = jnp.einsum(
        "bqhd,bkhd->bhqk", attended_grad, value_rows, preferred_element_type=jnp.float32
    )
    score_grad = prob_rows * (prob_grad - jnp.sum(prob_grad * prob_rows, axis=-1, keepdims=True))
    raw_grad = (score_grad * score_scale).astype(jnp.bfloat16)
    query_grad = jnp.einsum(
        "bhqk,bkhd->bqhd", raw_grad, key_rows, preferred_element_type=jnp.float32
    )
    key_grad = jnp.einsum(
        "bhqk,bqhd->bkhd", raw_grad, query_rows, preferred_element_type=jnp.float32
    )
    qkv_rows_grad = (
        jnp.stack([query_grad, key_grad, value_grad], axis=3)
        .astype(jnp.bfloat16)
        .reshape(row_count, 3 * model_width)
    )
    qkv_grad = jnp.einsum("td,tc->dc", first_low, qkv_rows_grad, preferred_element_type=jnp.float32)
    normed_grad = jnp.einsum(
        "tc,dc->td", qkv_rows_grad, qkv_full, preferred_element_type=jnp.float32
    )
    input_part, gain_one, shift_one = first_pull(normed_grad)
    input_grad = middle_grad + input_part
    norm_grad = jnp.stack([gain_one, shift_one, gain_two, shift_two], axis=0)
    qkv_owned, proj_owned, router_owned, norm_owned = (
        lax.psum_scatter(qkv_grad, ("expert", "head"), scatter_dimension=0, tiled=True),
        lax.psum_scatter(proj_grad, ("expert", "head"), scatter_dimension=0, tiled=True),
        lax.psum_scatter(router_grad, ("expert", "head"), scatter_dimension=0, tiled=True),
        lax.psum_scatter(norm_grad, ("expert", "head"), scatter_dimension=1, tiled=True),
    )
    qkv_new = adam_step(qkv_master, qkv_mean, qkv_square, qkv_owned, 2.0 * model_width ** (-0.5))
    proj_new = adam_step(
        proj_master, proj_mean, proj_square, proj_owned, 2.0 * (model_width // 16) ** (-0.5)
    )
    router_new = adam_step(
        router_master, router_mean, router_square, router_owned, 2.0 * (4 * model_width) ** (-0.5)
    )
    norm_new = adam_step(norm_master, norm_mean, norm_square, norm_owned, NORM_RATE)
    inner_new = adam_step(
        inner_master, inner_mean, inner_square, inner_grad, 2.0 * model_width ** (-0.5)
    )
    outer_new = adam_step(
        outer_master,
        outer_mean,
        outer_square,
        outer_grad,
        2.0 * max(1, FF * 4 // (expert_count * expert_count)) ** (-0.5),
    )
    return (
        block_output,
        input_grad,
        qkv_new[0],
        qkv_new[1],
        qkv_new[2],
        qkv_new[3],
        proj_new[0],
        proj_new[1],
        proj_new[2],
        proj_new[3],
        router_new[0],
        router_new[1],
        router_new[2],
        router_new[3],
        norm_new[0],
        norm_new[1],
        norm_new[2],
        norm_new[3],
        inner_new[0],
        inner_new[1],
        inner_new[2],
        inner_new[3],
        outer_new[0],
        outer_new[1],
        outer_new[2],
        outer_new[3],
    )


def solution(mesh):
    in_specs = (
        P(("expert", "head"), None),
        P(("expert", "head"), None),
        P(("expert", "head"), None),
        P(("expert", "head"), None),
        P(("expert", "head"), None),
        P(("expert", "head"), None),
        P(("expert", "head"), None),
        P(("expert", "head"), None),
        P(("expert", "head"), None),
        P(("expert", "head"), None),
        P(("expert", "head"), None),
        P(("expert", "head"), None),
        P(None, ("expert", "head")),
        P(None, ("expert", "head")),
        P(None, ("expert", "head")),
        P("expert", None, "head"),
        P("expert", None, "head"),
        P("expert", None, "head"),
        P("expert", "head", None),
        P("expert", "head", None),
        P("expert", "head", None),
    )
    out_specs = (
        P(("expert", "head"), None),
        P(("expert", "head"), None),
        P(("expert", "head"), None),
        P(("expert", "head"), None),
        P(("expert", "head"), None),
        P(("expert", "head"), None),
        P(("expert", "head"), None),
        P(("expert", "head"), None),
        P(("expert", "head"), None),
        P(("expert", "head"), None),
        P(("expert", "head"), None),
        P(("expert", "head"), None),
        P(("expert", "head"), None),
        P(("expert", "head"), None),
        P(None, ("expert", "head")),
        P(None, ("expert", "head")),
        P(None, ("expert", "head")),
        P(None, ("expert", "head")),
        P("expert", None, "head"),
        P("expert", None, "head"),
        P("expert", None, "head"),
        P("expert", None, "head"),
        P("expert", "head", None),
        P("expert", "head", None),
        P("expert", "head", None),
        P("expert", "head", None),
    )
    return jax.shard_map(
        on_device, mesh=mesh, in_specs=in_specs, out_specs=out_specs, check_vma=False
    )
```

profile of v0, /device:TPU:0, one launch (start us, length us, event | category | flops | bytes accessed | tf_op | source)
XLA Modules:
  0.0 1574.8 jit_solution(6014915333316710512)
XLA Ops:
  15.9 8.8 scatter_custom_fusion
  26.2 43.3 %all-gather = bf16[32,24,4]{1,2,0:T(4,128)(2,1)S(1)} all-gather(bf16[1,24,4]{1,2,0:T(4,128)(2,1)S(1)} %convert_bitcast_fusion.2), channel_id=1, replica_groups=mesh['expert'=8,'head'=4] {'expert','head'}, dimensions={0}, use_global_device_ids=true | all-gather | bytes 6336 | tf_op jit(solution)/shard_map/all_gather | solution.py:95
  69.9 4.4 all-gather.7.cloned.1.call-done
  74.4 7.4 convolution_convert_fusion.2
  81.8 18.2 %reshape.328 = bf16[4,197,12,3,64]{4,3,2,1,0:T(4,128)(2,1)} reshape(bf16[788,2304]{1,0:T(8,128)(2,1)} %convolution_convert_fusion.2) | data formatting | bytes 7262208 | tf_op jit(solution)/shard_map/reshape | solution.py:102
  100.0 20.9 %fusion.128 = (bf16[4,197,12,1,64]{4,3,2,1,0:T(2,128)(2,1)}, bf16[4,197,12,1,64]{4,3,2,1,0:T(2,128)(2,1)}, bf16[4,197,12,1,64]{4,3,2,1,0:T(2,128)(2,1)}) fusion(bf16[4,197,12,3,64]{4,3,2,1,0:T(4,128)(2,1)} %reshape.328), kind=kLoop, calls=%fused_computation.191 | loop fusion | bytes 7262208 | tf_op jit(solution)/shard_map/slice | solution.py:103
  120.9 10.8 copy.166
  131.7 10.8 copy.167
  142.5 9.4 copy.165
  152.0 4.0 multiply_reduce_fusion.1
  169.7 8.6 gather_fusion
  178.3 4.9 gather.10
  185.7 92.0 %all_to_all.20 = bf16[8,316,768]{2,1,0:T(8,128)(2,1)S(1)} all-to-all(bf16[8,316,768]{2,1,0:T(8,128)(2,1)S(1)} %broadcast_select_fusion), channel_id=1, replica_groups=mesh['expert'=8,'head'=4] {'expert'}, dimensions={0} | all-to-all | bytes 7766016 | tf_op jit(solution)/shard_map/all_to_all | solution.py:132
  277.7 4.0 copy.140
  281.8 97.1 %all-gather.11.cloned.1.call-done = bf16[32,316,768]{2,0,1:T(8,128)(2,1)} async-done(((bf16[8,316,768]{2,0,1:T(8,128)(2,1)}), bf16[32,316,768]{2,0,1:T(8,128)(2,1)}) %all-gather.11.cloned.1.call-update) | async-done | bytes 15532048 | tf_op jit(solution)/shard_map/all_gather | solution.py:135
  378.9 12.4 copy.141
  391.3 17.6 %reshape.257 = bf16[10112,768]{1,0:T(8,128)(2,1)} reshape(bf16[32,316,768]{2,1,0:T(8,128)(2,1)} %copy.141) | data formatting | bytes 31064064 | tf_op jit(solution)/shard_map/reshape | solution.py:135
  408.9 27.3 %multiply_convert_fusion = (bf16[10112,768]{1,0:T(8,128)(2,1)}, f32[10112,768]{1,0:T(8,128)}) fusion(bf16[10112,768]{1,0:T(8,128)(2,1)} %reshape.257, f32[1,768,768]{2,1,0:T(8,128)} %param.38), kind=kOutput, calls=%fused_computation.15 | convolution fusion | flops 11999084544 | bytes 64487424 | tf_op jit(solution)/shard_map/dot_general | solution.py:136
  436.2 17.6 %dot_general.74 = bf16[32,316,768]{2,1,0:T(8,128)(2,1)} reshape(bf16[10112,768]{1,0:T(8,128)(2,1)} %get-tuple-element.79) | data formatting | bytes 31064064 | tf_op jit(solution)/shard_map/dot_general | solution.py:139
  453.8 20.0 %convolution_convert_fusion.1 = bf16[32,316,768]{2,1,0:T(8,128)(2,1)} fusion(bf16[32,316,768]{2,1,0:T(8,128)(2,1)} %dot_general.74, f32[1,768,768]{2,1,0:T(8,128)} %param.41), kind=kOutput, calls=%fused_computation.17 | convolution fusion | flops 11936956416 | bytes 33423360 | tf_op jit(solution)/shard_map/dot_general | solution.py:139
  473.8 120.0 %reduce-scatter.7.cloned.1.call-done = bf16[8,316,768]{2,1,0:T(8,128)(2,1)} async-done(((bf16[32,316,768]{2,1,0:T(8,128)(2,1)}), bf16[8,316,768]{2,1,0:T(8,128)(2,1)}) %reduce-scatter.7.cloned.1.call-update) | async-done | bytes 3883024 | tf_op jit(solution)/shard_map/reduce_scatter | solution.py:142
  593.8 5.5 all-to-all-start.1
  599.4 99.8 %all-gather.1 = bf16[32,24,8]{1,2,0:T(8,128)(2,1)S(1)} all-gather(bf16[1,24,8]{1,2,0:T(8,128)(2,1)S(1)} %convert_bitcast_fusion.1), channel_id=1, replica_groups=mesh['expert'=8,'head'=4] {'expert','head'}, dimensions={0}, use_global_device_ids=true | all-gather | bytes 12672 | tf_op jit(solution)/shard_map/all_gather | solution.py:94
  699.3 3.4 mul.439
  702.7 7.5 mul.440
  711.4 4.8 reshape.258
  716.2 10.0 gather_fusion.1
  726.2 4.2 multiply_reduce_fusion.2
  731.4 20.0 %scatter_custom_fusion.1 = bf16[2528,768]{1,0:T(8,128)(2,1)} fusion(s32[1576]{0:T(1024)} %copy-done.65, f32[1576,768]{1,0:T(8,128)} %mul.440, f32[1576]{0:T(1024)S(1)} %mul.448, bf16[]{:T(256)} %constant.69.clone.1), kind=kCustom, calls=%fused_computation.62 | custom fusion | flops 2420736 | bytes 8731296 | tf_op jit(solution)/shard_map/scatter | solution.py:160
  751.4 4.8 reshape.259
  756.2 104.4 %all_to_all.21 = bf16[8,316,768]{2,1,0:T(8,128)(2,1)S(1)} all-to-all(bf16[8,316,768]{2,1,0:T(8,128)(2,1)} %reshape.259), channel_id=1, replica_groups=mesh['expert'=8,'head'=4] {'expert'}, dimensions={0} | all-to-all | bytes 7766016 | tf_op jit(solution)/shard_map/all_to_all | solution.py:162
  860.6 4.2 copy.144
  864.8 97.1 %all-gather.13.cloned.1.call-done = bf16[32,316,768]{2,0,1:T(8,128)(2,1)} async-done(((bf16[8,316,768]{2,0,1:T(8,128)(2,1)}), bf16[32,316,768]{2,0,1:T(8,128)(2,1)}) %all-gather.13.cloned.1.call-update) | async-done | bytes 15532048 | tf_op jit(solution)/shard_map/all_gather | solution.py:169
  961.9 12.2 copy.145
  974.1 17.8 %reshape.260 = bf16[10112,768]{1,0:T(8,128)(2,1)} reshape(bf16[32,316,768]{2,1,0:T(8,128)(2,1)} %copy.145) | data formatting | bytes 31064064 | tf_op jit(solution)/shard_map/reshape | solution.py:169
  991.9 35.1 %fusion.7 = bf16[10112,768]{1,0:T(8,128)(2,1)} fusion(f32[10112,768]{1,0:T(8,128)} %get-tuple-element.80, bf16[10112,768]{1,0:T(8,128)(2,1)} %reshape.260, f32[1,768,768]{2,1,0:T(8,128)S(1)} %copy-done.74), kind=kOutput, calls=%fused_computation.14 | convolution fusion | flops 12084510720 | bytes 64487424 | tf_op jit(solution)/shard_map/rd,fd->rf/dot_general | solution.py:172
  1027.0 17.8 %dot_general.78 = bf16[32,316,768]{2,1,0:T(8,128)(2,1)} reshape(bf16[10112,768]{1,0:T(8,128)(2,1)} %fusion.7) | data formatting | bytes 31064064 | tf_op jit(solution)/shard_map/rf,df->rd/dot_general | solution.py:182
  1044.7 21.3 %convolution_convert_fusion = bf16[32,316,768]{2,1,0:T(8,128)(2,1)} fusion(bf16[32,316,768]{2,1,0:T(8,128)(2,1)} %dot_general.78, f32[1,768,768]{2,1,0:T(8,128)S(1)} %copy-done.75), kind=kOutput, calls=%fused_computation.16 | convolution fusion | flops 11936956416 | bytes 33423360 | tf_op jit(solution)/shard_map/rf,df->rd/dot_general | solution.py:182
  1066.1 120.0 %reduce-scatter.9.cloned.1.call-done = bf16[8,316,768]{2,1,0:T(8,128)(2,1)} async-done(((bf16[32,316,768]{2,1,0:T(8,128)(2,1)}), bf16[8,316,768]{2,1,0:T(8,128)(2,1)}) %reduce-scatter.9.cloned.1.call-update) | async-done | bytes 3883024 | tf_op jit(solution)/shard_map/reduce_scatter | solution.py:185
  1186.1 5.5 all-to-all-start.3
  1191.8 87.5 %all-to-all-done.3 = bf16[8,316,768]{2,1,0:T(8,128)(2,1)} async-done(((bf16[8,316,768]{2,1,0:T(8,128)(2,1)}), bf16[8,316,768]{2,1,0:T(8,128)(2,1)}, u32[]{:S(2)}, u32[]{:S(2)}) %all-to-all-start.3) | async-done | bytes 3883040 | tf_op jit(solution)/shard_map/all_to_all | solution.py:188
  1279.2 4.8 reshape.261
  1284.1 10.2 gather_fusion.2
  1294.3 5.5 select_convert_fusion
  1299.8 6.9 reshape.268
  1306.7 9.7 multiply_reduce_fusion.3
  1316.4 7.1 reshape.269
  1323.5 9.7 reduce_sum.256
  1343.0 3.2 convolution_convert_fusion.5
  1346.3 3.7 reshape.329
  1349.9 4.2 copy.147
  1354.2 5.2 fusion.51
  1359.4 19.0 %fusion.58 = bf16[4,197,12,1,64]{1,4,2,0,3:T(8,128)(2,1)} fusion(f32[4,12,197,197]{2,3,1,0:T(8,128)} %fusion.51, f32[4,12,197]{2,1,0:T(8,128)S(1)} %copy-done.28, f32[4,12,197,197]{2,3,1,0:T(8,128)} %copy-done, bf16[4,197,12,1,64]{1,4,2,0,3:T(8,128)(2,1)} %copy.166), kind=kOutput, calls=%fused_computation.91 | convolution fusion | flops 255822816 | bytes 17361216 | tf_op jit(solution)/shard_map/bhqk,bqhd->bkhd/dot_general | solution.py:220
  1378.5 18.2 %fusion.63 = bf16[4,197,12,1,64]{1,4,2,0,3:T(8,128)(2,1)} fusion(f32[4,12,197,197]{2,3,1,0:T(8,128)} %fusion.51, f32[4,12,197]{2,1,0:T(8,128)S(1)} %copy-done.28, f32[4,12,197,197]{2,3,1,0:T(8,128)} %copy-done, bf16[4,197,12,1,64]{1,4,2,0,3:T(8,128)(2,1)S(1)} %copy-done.14), kind=kOutput, calls=%fused_computation.92 | convolution fusion | flops 255822816 | bytes 17361216 | tf_op jit(solution)/shard_map/bhqk,bkhd->bqhd/dot_general | solution.py:217
  1396.7 5.9 fusion.57
  1404.2 6.6 copy.152
  1410.8 9.7 convert_element_type.151
  1420.5 8.8 fusion.109
  1430.8 25.5 %fusion.113 = (bf16[1,768,768]{2,1,0:T(8,128)(2,1)}, f32[1,768,768]{2,1,0:T(8,128)}, f32[1,768,768]{2,1,0:T(8,128)}, f32[1,768,768]{2,1,0:T(8,128)}) fusion(f32[1,768,768]{2,1,0:T(8,128)} %param.41, f32[1,768,768]{2,1,0:T(8,128)} %param.42, f32[1,768,768]{2,1,0:T(8,128)} %param.43, bf16[10112,768]{1,0:T(8,128)(2,1)} %get-tuple-element.79, ...), kind=kOutput, calls=%fused_computation.184 | convolution fusion | flops 11937447936 | bytes 46399488 | tf_op jit(solution)/shard_map/rf,rd->fd/dot_general | solution.py:176
  1456.3 26.2 %fusion.116 = (bf16[1,768,768]{2,1,0:T(8,128)(2,1)}, f32[1,768,768]{2,1,0:T(8,128)}, f32[1,768,768]{2,1,0:T(8,128)}, f32[1,768,768]{2,1,0:T(8,128)}) fusion(f32[1,768,768]{2,1,0:T(8,128)} %param.38, f32[1,768,768]{2,1,0:T(8,128)} %param.39, f32[1,768,768]{2,1,0:T(8,128)} %param.40, bf16[10112,768]{1,0:T(8,128)(2,1)} %reshape.257, bf16[10112,768]{1,0:T(8,128)(2,1)} %fusion.7), kind=kOutput, calls=%fused_computation.185 | convolution fusion | flops 11937447936 | bytes 46399488 | tf_op jit(solution)/shard_map/rd,rf->df/dot_general | solution.py:179
  1482.5 7.2 fusion.30
  1492.7 39.8 %all-reduce.4 = (f32[768,8]{0,1:T(8,128)S(1)}, f32[4,768]{1,0:T(4,128)S(1)}) all-reduce(f32[768,8]{0,1:T(8,128)S(1)} %fusion.131, f32[4,768]{1,0:T(4,128)S(1)} %pad_maximum_fusion.1), channel_id=6, replica_groups=mesh['expert'=8,'head'=4] {'expert','head'}, use_global_device_ids=true, to_apply=%region_28.30.clone | all-reduce | flops 9216 | bytes 73728
  1534.0 4.1 add_add_fusion.2
  1539.7 26.1 %reduce-scatter.11.cloned.1.call-done = f32[24,2304]{1,0:T(8,128)} async-done(((f32[768,2304]{1,0:T(8,128)}), f32[24,2304]{1,0:T(8,128)}) %reduce-scatter.11.cloned.1.call-update) | async-done | bytes 221200 | tf_op jit(solution)/shard_map/reduce_scatter | solution.py:236
  (250 shorter events, 49.6 us)
Async XLA Ops:
  7.2 17.6 %copy-start.5 = (bf16[788,768]{1,0:T(8,128)(2,1)S(1)}, bf16[788,768]{1,0:T(8,128)(2,1)}, u32[]{:S(2)}) copy-start(bf16[788,768]{1,0:T(8,128)(2,1)} %param.23) | copy-start | bytes 3631108
  7.2 67.2 %all-gather.7.cloned.1.call-start = ((), (), s32[]{:S(2)}) async-start(), calls=%async_computation.8 | async-start | bytes 3649536 | tf_op jit(solution)/shard_map/all_gather | solution.py:92
  9.0 156.2 %all-gather.9.cloned.1.call-start = ((), (), s32[]{:S(2)}) async-start(), calls=%async_computation.9 | async-start | bytes 1216512 | tf_op jit(solution)/shard_map/all_gather | solution.py:93
  10.5 15.6 copy-start.66
  10.6 368.3 %all-gather.11.cloned.1.call-start = ((), (), s32[]{:S(2)}) async-start(), calls=%async_computation.10 | async-start | bytes 19415040 | tf_op jit(solution)/shard_map/all_gather | solution.py:135
  12.4 69.3 %copy-start.32 = (s32[1576]{0:T(1024)}, s32[1576]{0:T(1024)S(1)}, u32[]{:S(2)}) copy-start(s32[1576]{0:T(1024)S(1)} %eq.38) | copy-start | bytes 18916
  15.4 66.4 %copy-start.42 = (s32[1576]{0:T(1024)}, s32[1576]{0:T(1024)S(1)}, u32[]{:S(2)}) copy-start(s32[1576]{0:T(1024)S(1)} %fusion.88) | copy-start | bytes 18916
  15.9 9.7 copy-start.65
  25.0 56.7 %copy-start.48 = (f32[788]{0:T(1024)}, f32[788]{0:T(1024)S(1)}, u32[]{:S(2)}) copy-start(f32[788]{0:T(1024)S(1)} %broadcast_multiply_fusion.2) | copy-start | bytes 9460
  26.2 55.6 %copy-start.55 = (f32[788]{0:T(1024)}, f32[788]{0:T(1024)S(1)}, u32[]{:S(2)}) copy-start(f32[788]{0:T(1024)S(1)} %fusion.98) | copy-start | bytes 9460
  69.8 12.0 copy-start.53
  69.8 12.0 copy-start.70
  69.8 98.9 %copy-start.44 = (f32[768]{0:T(1024)}, f32[768]{0:T(1024)S(1)}, u32[]{:S(2)}) copy-start(f32[768]{0:T(1024)S(1)} %get-tuple-element.33) | copy-start | bytes 9220
  151.9 6.1 copy-start.9
  169.6 540.7 %copy-start.7 = (bf16[788,768]{1,0:T(8,128)(2,1)}, bf16[788,768]{1,0:T(8,128)(2,1)S(1)}, u32[]{:S(2)}) copy-start(bf16[788,768]{1,0:T(8,128)(2,1)S(1)} %add_convert_fusion.1) | copy-start | bytes 3631108
  281.7 312.1 %reduce-scatter.7.cloned.1.call-start = ((), (), s32[]{:S(2)}) async-start(), calls=%async_computation.11 | async-start | bytes 19660800 | tf_op jit(solution)/shard_map/reduce_scatter | solution.py:142
  473.8 125.6 %copy-start.63 = (f32[24,8]{0,1:T(8,128)S(1)}, f32[24,8]{0,1:T(8,128)}, u32[]{:S(2)}) copy-start(f32[24,8]{0,1:T(8,128)} %param.32) | copy-start | bytes 2308
  473.8 225.5 %copy-start.15 = (bf16[788,768]{1,0:T(8,128)(2,1)S(1)}, bf16[788,768]{1,0:T(8,128)(2,1)}, u32[]{:S(2)}) copy-start(bf16[788,768]{1,0:T(8,128)(2,1)} %param.24) | copy-start | bytes 3631108
  593.8 117.6 %all-to-all-start.1 = ((bf16[8,316,768]{2,1,0:T(8,128)(2,1)}), bf16[8,316,768]{2,1,0:T(8,128)(2,1)}, u32[]{:S(2)}, u32[]{:S(2)}) async-start(bf16[8,316,768]{2,1,0:T(8,128)(2,1)} %reduce-scatter.7.cloned.1.call-done), calls=%async_computation.2 | async-start | bytes 7864320 | tf_op jit(solution)/shard_map/all_to_all | solution.py:145
  599.3 362.6 %all-gather.13.cloned.1.call-start = ((), (), s32[]{:S(2)}) async-start(), calls=%async_computation.12 | async-start | bytes 19415040 | tf_op jit(solution)/shard_map/all_gather | solution.py:169
  699.3 11.0 copy-start.34
  702.7 7.5 copy-start.33
  702.7 7.5 copy-start.43
  710.3 15.9 %copy-start.61 = (pred[1576]{0:T(1024)(128)(4,1)}, pred[1576]{0:T(1024)(128)(4,1)S(1)}, u32[]{:S(2)}) copy-start(pred[1576]{0:T(1024)(128)(4,1)S(1)} %get-tuple-element.67) | copy-start | bytes 4732
  710.8 5.4 copy-start.38
  711.4 4.8 copy-start.50
  731.2 20.2 %copy-start.19 = (f32[788,2]{1,0:T(8,128)}, f32[788,2]{1,0:T(8,128)S(1)}, u32[]{:S(2)}) copy-start(f32[788,2]{1,0:T(8,128)S(1)} %copy.136) | copy-start | bytes 18916
  864.8 321.3 %reduce-scatter.9.cloned.1.call-start = ((), (), s32[]{:S(2)}) async-start(), calls=%async_computation.13 | async-start | bytes 19660800 | tf_op jit(solution)/shard_map/reduce_scatter | solution.py:185
  974.1 17.8 %copy-start.74 = (f32[1,768,768]{2,1,0:T(8,128)S(1)}, f32[1,768,768]{2,1,0:T(8,128)}, u32[]{:S(2)}) copy-start(f32[1,768,768]{2,1,0:T(8,128)} %param.41) | copy-start | bytes 7077892
  1026.9 17.8 %copy-start.75 = (f32[1,768,768]{2,1,0:T(8,128)S(1)}, f32[1,768,768]{2,1,0:T(8,128)}, u32[]{:S(2)}) copy-start(f32[1,768,768]{2,1,0:T(8,128)} %param.38) | copy-start | bytes 7077892
  1066.1 125.6 %copy-start.51 = (f32[788]{0:T(1024)S(1)}, f32[788]{0:T(1024)}, u32[]{:S(2)}) copy-start(f32[788]{0:T(1024)} %copy-done.50) | copy-start | bytes 9460
  1066.1 125.6 %copy-start.26 = (f32[788,8]{0,1:T(8,128)S(1)}, f32[788,8]{0,1:T(8,128)}, u32[]{:S(2)}) copy-start(f32[788,8]{0,1:T(8,128)} %copy-done.25) | copy-start | bytes 75652
  1066.1 125.6 %copy-start.39 = (f32[788]{0:T(1024)S(1)}, f32[788]{0:T(1024)}, u32[]{:S(2)}) copy-start(f32[788]{0:T(1024)} %copy-done.38) | copy-start | bytes 9460
  1186.1 93.2 %all-to-all-start.3 = ((bf16[8,316,768]{2,1,0:T(8,128)(2,1)}), bf16[8,316,768]{2,1,0:T(8,128)(2,1)}, u32[]{:S(2)}, u32[]{:S(2)}) async-start(bf16[8,316,768]{2,1,0:T(8,128)(2,1)} %reduce-scatter.9.cloned.1.call-done), calls=%async_computation.5 | async-start | bytes 7864320 | tf_op jit(solution)/shard_map/all_to_all | solution.py:188
  1191.6 346.5 %reduce-scatter.13.cloned.1.call-start = ((), (), s32[]{:S(2)}) async-start(), calls=%async_computation.15 | async-start | bytes 2433024 | tf_op jit(solution)/shard_map/reduce_scatter | solution.py:237
  1284.0 10.2 copy-start.4
  1284.0 10.2 copy-start.62
  1299.8 6.9 copy-start.20
  1323.5 9.7 copy-start.2
  1323.5 9.7 copy-start.35
  1323.5 9.7 copy-start.37
  1323.5 9.7 copy-start.45
  1323.5 9.7 copy-start.47
  1343.0 222.9 %reduce-scatter.11.cloned.1.call-start = ((), (), s32[]{:S(2)}) async-start(), calls=%async_computation.14 | async-start | bytes 7299072 | tf_op jit(solution)/shard_map/reduce_scatter | solution.py:236
  1354.2 5.2 copy-start.28
  1359.4 19.1 %copy-start.14 = (bf16[4,197,12,1,64]{1,4,2,0,3:T(8,128)(2,1)S(1)}, bf16[4,197,12,1,64]{1,4,2,0,3:T(8,128)(2,1)}, u32[]{:S(2)}) copy-start(bf16[4,197,12,1,64]{1,4,2,0,3:T(8,128)(2,1)} %copy.167) | copy-start | bytes 3631108
  1396.7 6.0 copy-start.21
  1396.7 6.0 copy-start.22
  1410.8 9.7 copy-start.6
  1410.8 9.7 copy-start.49
  1410.8 9.7 copy-start.54
  1410.8 9.7 copy-start.56
  1410.8 9.7 copy-start.71
  1482.5 7.3 copy-start.58
  1489.8 42.7 %copy-start.67 = (f32[4,24]{1,0:T(4,128)S(1)}, f32[4,24]{1,0:T(4,128)}, u32[]{:S(2)}) copy-start(f32[4,24]{1,0:T(4,128)} %param.35) | copy-start | bytes 1156
  1489.8 42.7 %copy-start.72 = (f32[4,24]{1,0:T(4,128)S(1)}, f32[4,24]{1,0:T(4,128)}, u32[]{:S(2)}) copy-start(f32[4,24]{1,0:T(4,128)} %param.36) | copy-start | bytes 1156
  1489.8 42.7 %copy-start.73 = (f32[4,24]{1,0:T(4,128)S(1)}, f32[4,24]{1,0:T(4,128)}, u32[]{:S(2)}) copy-start(f32[4,24]{1,0:T(4,128)} %param.37) | copy-start | bytes 1156
  1489.8 43.4 %copy-start.64 = (f32[24,8]{0,1:T(8,128)S(1)}, f32[24,8]{0,1:T(8,128)}, u32[]{:S(2)}) copy-start(f32[24,8]{0,1:T(8,128)} %param.32) | copy-start | bytes 2308
  1489.8 43.4 %copy-start.68 = (f32[24,8]{0,1:T(8,128)S(1)}, f32[24,8]{0,1:T(8,128)}, u32[]{:S(2)}) copy-start(f32[24,8]{0,1:T(8,128)} %param.33) | copy-start | bytes 2308
  1489.8 43.4 %copy-start.69 = (f32[24,8]{0,1:T(8,128)S(1)}, f32[24,8]{0,1:T(8,128)}, u32[]{:S(2)}) copy-start(f32[24,8]{0,1:T(8,128)} %param.34) | copy-start | bytes 2308
  1489.9 44.1 %copy-start.18 = (bf16[788,768]{1,0:T(8,128)(2,1)S(1)}, bf16[788,768]{1,0:T(8,128)(2,1)}, u32[]{:S(2)}) copy-start(bf16[788,768]{1,0:T(8,128)(2,1)} %param.24) | copy-start | bytes 3631108
  1533.9 31.9 %copy-start.24 = (f32[24,2304]{1,0:T(8,128)S(1)}, f32[24,2304]{1,0:T(8,128)}, u32[]{:S(2)}) copy-start(f32[24,2304]{1,0:T(8,128)} %param.26) | copy-start | bytes 663556
  1533.9 31.9 %copy-start.30 = (f32[24,2304]{1,0:T(8,128)S(1)}, f32[24,2304]{1,0:T(8,128)}, u32[]{:S(2)}) copy-start(f32[24,2304]{1,0:T(8,128)} %param.27) | copy-start | bytes 663556
  1534.0 31.9 %copy-start.31 = (f32[24,2304]{1,0:T(8,128)S(1)}, f32[24,2304]{1,0:T(8,128)}, u32[]{:S(2)}) copy-start(f32[24,2304]{1,0:T(8,128)} %param.28) | copy-start | bytes 663556
  (22 other events, 58.2 us)
Sparse Core Ops, SparseCore 0:
  11.5 62.8 all-gather.6
  77.9 52.8 all-gather.8
  281.8 96.9 all-gather.10
  473.9 119.8 reduce-scatter.6
  864.9 96.9 all-gather.12
  1066.2 119.8 reduce-scatter.8
  1343.1 97.1 reduce-scatter.12
  1446.9 118.9 reduce-scatter.10
where the time goes:
time: 1580 us; the launch traced here: 1570 us
  waiting for transfers between devices  552 us (35%)
  blocking collectives  379 us (24%)
  local copies, waits for them, and re-layouts  294 us (19%)
  matrix products  246 us (16%)
  other arithmetic  76.1 us (5%)
    reduce_scatter x1, waiting for transfers between devices, on_device(): lax.psum_scatter(partial_value.astype(jnp.bfloat16), 'head', scatter_dime...  120 us
    reduce_scatter x1, waiting for transfers between devices, on_device(): lax.psum_scatter(row_partial.astype(jnp.bfloat16), 'head', scatter_dimens...  120 us
    all_to_all x1, blocking collectives, on_device(): lax.all_to_all(slot_grads.reshape(expert_count, capacity, model_width), '...  104 us
    all_gather x1, blocking collectives, on_device(): lax.all_gather(router_master.astype(jnp.bfloat16), ('expert', 'head'), ax...  99.8 us
    all_gather x1, waiting for transfers between devices, on_device(): lax.all_gather(owner_grads, 'head', axis=0, tiled=True)  97.1 us
    all_gather x1, waiting for transfers between devices, on_device(): lax.all_gather(arrived, 'head', axis=0, tiled=True).reshape(-1, model_width)  97.1 us
    all_to_all x1, blocking collectives, on_device(): lax.all_to_all(outgoing, 'expert', split_axis=0, concat_axis=0, tiled=True)  92 us
    all_to_all x1, waiting for transfers between devices, on_device(): lax.all_to_all(row_grads, 'expert', split_axis=0, concat_axis=0, tiled=True)  87.5 us
  transfers between devices with their start and end apart: 10, of which 7 were waited for; matrix products, arithmetic and copies ran while one was open for 17% of the time, Pallas kernels for 0%

commit v1 on v0

v1 whole, which is shorter than its diff:
```python
import functools

import jax
import jax.numpy as jnp
from jax import lax
from jax.experimental import pallas as pl
from jax.experimental.pallas import tpu as pltpu
from jax.sharding import PartitionSpec as P

HD = 64
FF = 3072
SEQ = 197
PAD = 208
STEP = 3

EPS_NORM = 1e-06
BETA_ONE = 0.5
BETA_TWO = 0.5
EPS_ADAM = 1e-08
DECAY = 0.1
NORM_RATE = 0.3

AXES = ("expert", "head")
F32 = jnp.float32
BF16 = jnp.bfloat16
VMEM_BYTES = 60 * 2**20
MESH = pl.DeviceIdType.MESH


def adam_step(master, first_state, square, gradient, step_rate):
    momentum = BETA_ONE * first_state + (1.0 - BETA_ONE) * gradient
    variance = BETA_TWO * square + (1.0 - BETA_TWO) * gradient * gradient
    first_fix = momentum / (1.0 - BETA_ONE**STEP)
    second_fix = variance / (1.0 - BETA_TWO**STEP)
    updated = master - step_rate * (first_fix / (jnp.sqrt(second_fix) + EPS_ADAM) + DECAY * master)
    return (updated, momentum, variance, updated.astype(BF16))


def dot_nn(a, b):
    return lax.dot_general(a, b, (((1,), (0,)), ((), ())), preferred_element_type=F32)


def dot_nt(a, b):
    return lax.dot_general(a, b, (((1,), (1,)), ((), ())), preferred_element_type=F32)


def dot_tn(a, b):
    return lax.dot_general(a, b, (((0,), (0,)), ((), ())), preferred_element_type=F32)


def cost(microseconds):
    return pl.CostEstimate(
        flops=int(microseconds * 1.1e9), bytes_accessed=int(microseconds * 3e6), transcendentals=0
    )


def params(**kw):
    return pltpu.CompilerParams(vmem_limit_bytes=VMEM_BYTES, **kw)


def spot_of(expert_axis, half, part, low):
    quarter = expert_axis // 4
    a, b, c = part // (2 * quarter), (part // quarter) % 2, part % quarter
    return (half * (expert_axis // 2) + a * quarter + c) * 4 + ((a + b + half) % 2) * 2 + low


def row_perm(expert_axis, k):
    return [
        (spot_of(expert_axis, r, f, lo), spot_of(expert_axis, r, f ^ k, lo))
        for r in range(2)
        for lo in range(2)
        for f in range(expert_axis)
    ]


def weight_perm(expert_axis, k):
    return [
        (f * 4 + h, spot_of(expert_axis, (h // 2) ^ k, f, h % 2))
        for f in range(expert_axis)
        for h in range(4)
    ]


def turned(perm):
    return [(b, a) for a, b in perm]


def core_perm(expert_axis):
    return [(d, d ^ 1) for d in range(expert_axis * 4)]


def routing_kernel(ids_ref, wide_ref, tall_ref, wide_out, tall_out, *, experts, cap):
    tokens = wide_ref.shape[1]
    part = ids_ref[0]
    row = lax.broadcasted_iota(jnp.int32, (tokens, tokens), 0)
    col = lax.broadcasted_iota(jnp.int32, (tokens, tokens), 1)

    wide = wide_ref[...] ^ part
    names = lax.broadcasted_iota(jnp.int32, (experts, tokens), 0)
    first, second = wide[0:1, :] == names, wide[1:2, :] == names
    seen = (first | second).astype(F32)
    before = dot_nn(seen.astype(BF16), (row < col).astype(BF16))
    place = jnp.concatenate(
        [
            jnp.sum(jnp.where(first, before, 0.0), axis=0, keepdims=True),
            jnp.sum(jnp.where(second, before, 0.0), axis=0, keepdims=True),
        ],
        axis=0,
    ).astype(jnp.int32)
    wide_out[...] = jnp.where(wide_ref[...] < 0, -1, wide * cap + place)

    tall = tall_ref[...] ^ part
    names = lax.broadcasted_iota(jnp.int32, (tokens, experts), 1)
    first, second = tall[:, 0:1] == names, tall[:, 1:2] == names
    seen = (first | second).astype(F32)
    before = dot_nn((col < row).astype(BF16), seen.astype(BF16))
    place = jnp.concatenate(
        [
            jnp.sum(jnp.where(first, before, 0.0), axis=1, keepdims=True),
            jnp.sum(jnp.where(second, before, 0.0), axis=1, keepdims=True),
        ],
        axis=1,
    ).astype(jnp.int32)
    tall_out[...] = jnp.where(tall_ref[...] < 0, -1, tall * cap + place)


def where_am_i(experts):
    quarter = experts // 4
    at_expert, at_head = lax.axis_index("expert"), lax.axis_index("head")
    half = lax.div(at_expert, experts // 2)
    rest = lax.rem(at_expert, experts // 2)
    a = lax.div(rest, quarter)
    b = lax.rem(lax.div(at_head, 2) + a + half, 2)
    return a * 2 * quarter + b * quarter + lax.rem(rest, quarter), half, lax.rem(at_head, 2)


def flipped(experts, part, k):
    there, bit = jnp.int32(0), 1
    while bit < experts:
        there = there + lax.rem(lax.div(part, bit) + lax.div(jnp.int32(k), bit), 2) * bit
        bit = bit * 2
    return there


def partner(experts, part, half, low, k):
    quarter = experts // 4
    there = flipped(experts, part, k)
    a = lax.div(there, 2 * quarter)
    row = half * (experts // 2) + a * quarter + lax.rem(there, quarter)
    return (row, lax.rem(lax.div(there, quarter) + a + half, 2) * 2 + low)


def block_at(experts, j):
    far = experts // 2
    if isinstance(j, int):
        return far if j == 0 else 0 if j == 1 else j + far - 1 if j <= far else j - far
    return jnp.where(
        j == 0, far, jnp.where(j == 1, 0, jnp.where(j <= far, j + far - 1, j - far))
    )


def greet(devices):
    barrier = pltpu.get_barrier_semaphore()
    for device in devices:
        pl.semaphore_signal(barrier, inc=1, device_id=device, device_id_type=MESH)
    pl.semaphore_wait(barrier, len(devices))


def picked_rows(wide_ref, rows, k, cap):
    slot = lax.broadcasted_iota(jnp.int32, (cap, rows.shape[0]), 0)
    first = wide_ref[0:1, :] - k * cap
    second = wide_ref[1:2, :] - k * cap
    pick = ((first == slot) | (second == slot)).astype(F32).astype(BF16)
    return dot_nn(pick, rows).astype(BF16)


def my_bits(count, index):
    return [lax.rem(lax.div(index, 2 ** (count - 1 - d)), 2) for d in range(count)]


def across(bits, low, d):
    place = jnp.int32(0)
    for i, bit in enumerate(bits):
        place = place * 2 + (1 - bit if i == d else bit)
    place = place * 2 + low
    return (lax.div(place, 4), lax.rem(place, 4))


def region(bits, full, d=None, flipped=False):
    return tuple(
        slice(None) if i in full else (1 - bit if (flipped and i == d) else bit)
        for i, bit in enumerate(bits)
    )


def parts_of(half_width):
    tiles = half_width // 128
    first = -(-tiles // 2) * 128
    return (slice(0, first), slice(first, half_width))


def gather_kernel(
    own_ref,
    wall_ref,
    twin,
    wall,
    twin_sem,
    step_send,
    step_recv,
    pass_send,
    pass_recv,
    own_sem,
):
    at_expert, at_head = lax.axis_index("expert"), lax.axis_index("head")
    low = lax.rem(at_head, 2)
    count = wall.ndim - 3
    bits = my_bits(count, lax.div(at_expert * 4 + at_head, 2))
    sibling = (at_expert, at_head + 1 - 2 * low)
    greet([sibling] + [across(bits, low, d) for d in range(count)])
    twin_copy = pltpu.make_async_remote_copy(
        src_ref=own_ref,
        dst_ref=twin,
        send_sem=twin_sem.at[0],
        recv_sem=twin_sem.at[1],
        device_id=sibling,
        device_id_type=MESH,
    )
    twin_copy.start()
    own_rows = own_ref.shape[0]
    half_width = wall.shape[-1]
    mine = tuple(bits)
    cols = parts_of(half_width)
    orders = (list(range(count)), list(range(count - 2)) + [count - 1, count - 2])

    def step_copy(q, i):
        full, d = set(orders[q][:i]), orders[q][i]
        at = (low,) + region(bits, full) + (slice(None), cols[q])
        return pltpu.make_async_remote_copy(
            src_ref=wall.at[at],
            dst_ref=wall.at[at],
            send_sem=step_send.at[q, i],
            recv_sem=step_recv.at[q, i],
            device_id=across(bits, low, d),
            device_id_type=MESH,
        )

    def pass_copy(q, i):
        full, d = set(orders[q][:i]), orders[q][i]
        at = (low,) + region(bits, full, d, True) + (slice(None), cols[q])
        return pltpu.make_async_remote_copy(
            src_ref=wall.at[at],
            dst_ref=wall.at[at],
            send_sem=pass_send.at[q, i],
            recv_sem=pass_recv.at[q, i],
            device_id=sibling,
            device_id_type=MESH,
        )

    twin_copy.wait()
    first = low == 0
    for side in range(2):
        at = slice(side * half_width, (side + 1) * half_width)
        ours, theirs = own_ref[:, at], twin[:, at]
        wall[(side,) + mine] = jnp.concatenate(
            [jnp.where(first, ours, theirs), jnp.where(first, theirs, ours)], axis=0
        ).astype(BF16)
    for i in range(count):
        for q in range(2):
            if i:
                step_copy(q, i - 1).wait_recv()
            step_copy(q, i).start()
        for q in range(2):
            if i:
                pass_copy(q, i - 1).start()
    for q in range(2):
        step_copy(q, count - 1).wait_recv()
        pass_copy(q, count - 1).start()
    for i in range(count):
        for q in range(2):
            step_copy(q, i).wait_send()
            pass_copy(q, i).wait()
    wall_copy = pltpu.make_async_copy(wall, wall_ref, own_sem)
    wall_copy.start()
    wall_copy.wait()


def reduce_kernel(
    all_ref,
    out_ref,
    total,
    landed,
    last,
    spare,
    pair_sem,
    step_send,
    step_recv,
    last_sem,
    *landings,
):
    at_expert, at_head = lax.axis_index("expert"), lax.axis_index("head")
    low = lax.rem(at_head, 2)
    count = all_ref.ndim - 3
    bits = my_bits(count, lax.div(at_expert * 4 + at_head, 2))
    sibling = (at_expert, at_head + 1 - 2 * low)
    greet([sibling] + [across(bits, low, d) for d in range(count)])
    half_width = all_ref.shape[-1]
    cols = parts_of(half_width)
    backwards = list(range(count))[::-1]
    orders = (backwards, [backwards[1], backwards[0]] + backwards[2:])

    def pair_copy(q):
        at = (slice(None),) * count + (slice(None), cols[q])
        return pltpu.make_async_remote_copy(
            src_ref=all_ref.at[(1 - low,) + at],
            dst_ref=landed.at[at],
            send_sem=pair_sem.at[q],
            recv_sem=pair_sem.at[2 + q],
            device_id=sibling,
            device_id_type=MESH,
        )

    def step_copy(q, i):
        gone, d = orders[q][:i], orders[q][i]
        full = set(range(count)) - set(gone) - {d}
        at = region(bits, full, d, True) + (slice(None), cols[q])
        return pltpu.make_async_remote_copy(
            src_ref=total.at[at],
            dst_ref=landings[q * count + i],
            send_sem=step_send.at[q, i],
            recv_sem=step_recv.at[q, i],
            device_id=across(bits, low, d),
            device_id_type=MESH,
        )

    for q in range(2):
        pair_copy(q).start()
    for q in range(2):
        at = (slice(None),) * count + (slice(None), cols[q])
        pair_copy(q).wait_recv()
        total[at] = (all_ref[(low,) + at].astype(F32) + landed[at].astype(F32)).astype(BF16)
        step_copy(q, 0).start()
    for i in range(count):
        for q in range(2):
            step_copy(q, i).wait_recv()
            gone, d = orders[q][:i], orders[q][i]
            full = set(range(count)) - set(gone) - {d}
            at = region(bits, full) + (slice(None), cols[q])
            added = total[at].astype(F32) + landings[q * count + i][...].astype(F32)
            if i < count - 1:
                total[at] = added.astype(BF16)
                step_copy(q, i + 1).start()
            else:
                last[:, cols[q]] = added
    own_rows = out_ref.shape[0]
    top, bottom = last[0:own_rows, :], last[own_rows:, :]
    first = low == 0
    spare[0] = jnp.where(first, bottom, top)
    last_copy = pltpu.make_async_remote_copy(
        src_ref=spare.at[0],
        dst_ref=spare.at[1],
        send_sem=last_sem.at[0],
        recv_sem=last_sem.at[1],
        device_id=sibling,
        device_id_type=MESH,
    )
    last_copy.start()
    ours = jnp.where(first, top, bottom)
    last_copy.wait()
    theirs = spare[1]
    out_ref[:, 0:half_width] = jnp.where(first, ours, theirs)
    out_ref[:, half_width:] = jnp.where(first, theirs, ours)
    for q in range(2):
        pair_copy(q).wait_send()
        for i in range(count):
            step_copy(q, i).wait_send()


def norm_parts(values):
    centered = values - jnp.mean(values, axis=-1, keepdims=True)
    spread = lax.rsqrt(jnp.mean(centered * centered, axis=-1, keepdims=True) + EPS_NORM)
    return centered * spread, spread


def norm_back(grad, unit, spread, gain):
    scaled = grad * gain
    return spread * (
        scaled
        - jnp.mean(scaled, axis=-1, keepdims=True)
        - unit * jnp.mean(scaled * unit, axis=-1, keepdims=True)
    )


def forward_kernel(
    x_ref,
    wall_ref,
    wide_ref,
    gy_ref,
    qkv_ref,
    o_ref,
    h_ref,
    n2_ref,
    p_ref,
    out_ref,
    small,
    held,
    send_sem,
    recv_sem,
    own_sem,
    *,
    experts,
    cap,
):
    width = x_ref.shape[2]
    part, half, low = where_am_i(experts)

    def swap_copy(k):
        return pltpu.make_async_remote_copy(
            src_ref=held.at[k],
            dst_ref=out_ref.at[k],
            send_sem=send_sem.at[k],
            recv_sem=recv_sem.at[k],
            device_id=partner(experts, part, half, low, k),
            device_id_type=MESH,
        )

    own_copy = pltpu.make_async_copy(held.at[0], out_ref.at[0], own_sem)

    @pl.when(pl.program_id(0) == 0)
    def _():
        greet([partner(experts, part, half, low, k) for k in range(1, experts)])
        rows = gy_ref[...]
        for k in range(experts - 1, 0, -1):
            held[k] = picked_rows(wide_ref, rows, k, cap)
            swap_copy(k).start()
        held[0] = picked_rows(wide_ref, rows, 0, cap)
        own_copy.start()
        small[...] = wall_ref[0, :, 2 * width :].astype(F32).T

    x = x_ref[0].astype(F32)
    gain, shift = small[experts : experts + 1, :], small[experts + 1 : experts + 2, :]
    unit, _ = norm_parts(x)
    n1 = (unit * gain + shift).astype(BF16)
    for j in range(3):
        qkv_ref[0, :, j * width : (j + 1) * width] = dot_nn(
            n1, wall_ref[j // 2, :, (j % 2) * width : (j % 2 + 1) * width]
        ).astype(BF16)
    lane = lax.broadcasted_iota(jnp.int32, (PAD, 128), 1)
    key_at = lax.broadcasted_iota(jnp.int32, (PAD, PAD), 1)
    for pair in range(width // 128):
        q = qkv_ref[0, :, pair * 128 : (pair + 1) * 128]
        k = qkv_ref[0, :, width + pair * 128 : width + (pair + 1) * 128]
        v = qkv_ref[0, :, 2 * width + pair * 128 : 2 * width + (pair + 1) * 128]
        halves = []
        for side in range(2):
            mine = (lane < HD) if side == 0 else (lane >= HD)
            scores = dot_nt(jnp.where(mine, q, jnp.zeros_like(q)), k) * (HD**-0.5)
            scores = jnp.where(key_at < SEQ, scores, -1e30)
            expo = jnp.exp(scores - jnp.max(scores, axis=-1, keepdims=True))
            probs = expo / jnp.sum(expo, axis=-1, keepdims=True)
            halves.append(dot_nn(probs.astype(BF16), v))
        o_ref[0, :, pair * 128 : (pair + 1) * 128] = jnp.where(
            lane < HD, halves[0], halves[1]
        ).astype(BF16)
    h = x + dot_nn(o_ref[0], wall_ref[1, :, width : 2 * width])
    h_ref[0] = h
    gain, shift = small[experts + 2 : experts + 3, :], small[experts + 3 : experts + 4, :]
    unit, _ = norm_parts(h)
    n2 = (unit * gain + shift).astype(BF16)
    n2_ref[0] = n2
    logits = dot_nt(small[0:experts, :].astype(BF16), n2)
    expo = jnp.exp(logits - jnp.max(logits, axis=0, keepdims=True))
    p_ref[0] = expo / jnp.sum(expo, axis=0, keepdims=True)

    @pl.when(pl.program_id(0) == pl.num_programs(0) - 1)
    def _():
        for k in range(1, experts):
            swap_copy(k).wait()
        own_copy.wait()


def expert_kernel(
    wide_ref,
    rows_ref,
    g_ref,
    w0_ref,
    w1_ref,
    w2_ref,
    w3_ref,
    router_ref,
    y_ref,
    dr_ref,
    in0_ref,
    out0_ref,
    in1_ref,
    out1_ref,
    x_all,
    g_all,
    held,
    w_all,
    acc,
    y_acc,
    dr_acc,
    x_send,
    x_recv,
    y_sem,
    dr_send,
    dr_recv,
    g_sem,
    w_sem,
    own_sem,
    pair_sem,
    ready_sem,
    *,
    experts,
    cap,
    group,
):
    part, half, low = where_am_i(experts)
    at_expert, at_head = lax.axis_index("expert"), lax.axis_index("head")
    sibling = (at_expert, at_head + 1 - 2 * low)
    greet([partner(experts, part, half, low, k) for k in range(1, experts)] + [sibling])
    sequence = [block_at(experts, j) for j in range(experts)]
    width = x_all.shape[2]
    slice_width = w_all.shape[2]
    tile = group * cap

    def x_copy(k):
        return pltpu.make_async_remote_copy(
            src_ref=held.at[k],
            dst_ref=x_all.at[k, pl.ds(0, cap), :],
            send_sem=x_send.at[k],
            recv_sem=x_recv.at[k],
            device_id=partner(experts, part, half, low, k),
            device_id_type=MESH,
        )

    def y_copy(k):
        return pltpu.make_async_copy(g_all.at[k], y_ref.at[k], y_sem.at[k])

    def dr_copy(k):
        return pltpu.make_async_remote_copy(
            src_ref=x_all.at[k],
            dst_ref=dr_ref.at[k],
            send_sem=dr_send.at[k],
            recv_sem=dr_recv.at[k],
            device_id=partner(experts, part, half, low, k),
            device_id_type=MESH,
        )

    weights = [
        pltpu.make_async_copy(w, w_all.at[j], w_sem.at[j])
        for j, w in enumerate((w0_ref, w1_ref, w2_ref, w3_ref))
    ]
    for copy in weights:
        copy.start()
    g_copy = pltpu.make_async_copy(g_ref, g_all, g_sem)
    g_copy.start()
    rows = rows_ref[...]
    for k in sequence:
        if k:
            held[k] = picked_rows(wide_ref, rows, k, cap)
            x_copy(k).start()
    x_all[0, 0:cap, :] = picked_rows(wide_ref, rows, 0, cap)
    acc[...] = jnp.zeros_like(acc)
    g_copy.wait()
    for copy in weights:
        copy.wait()

    def one_tile(t, _):
        base = t * group
        names = [block_at(experts, base + j) for j in range(group)]
        for k in names:

            @pl.when(k > 0)
            def _(k=k):
                x_copy(k).wait_recv()

        x = jnp.concatenate([x_all[k, 0:cap, :] for k in names], axis=0)
        g = jnp.concatenate([g_all[k] for k in names], axis=0)
        logits = dot_nt(x, router_ref[...])
        expo = jnp.exp(logits - jnp.max(logits, axis=-1, keepdims=True))
        probs = expo / jnp.sum(expo, axis=-1, keepdims=True)
        name = lax.broadcasted_iota(jnp.int32, probs.shape, 1)
        gate = jnp.sum(jnp.where(name == part, probs, 0.0), axis=-1, keepdims=True)
        dy = (gate * g.astype(F32)).astype(BF16)
        x_turned, dy_turned = x.T, dy.T

        def first(s):
            w_in = w_all[s, 0:width, :]
            w_out = w_all[s, width : 2 * width, :]
            acts, dus = [], []
            for i in range(0, slice_width, 256):
                u = dot_nn(x, w_in[:, i : i + 256])
                da = dot_nt(dy, w_out[i : i + 256, :])
                root = 0.7978845608028654
                sq = u * u
                th = jnp.tanh(u * (root + (root * 0.044715) * sq))
                plus = 0.5 + 0.5 * th
                acts.append((u * plus).astype(BF16))
                slope = plus + (0.5 * u) * (1.0 - th * th) * (root + (3.0 * root * 0.044715) * sq)
                dus.append((da * slope).astype(BF16))
            return jnp.concatenate(acts, axis=1), jnp.concatenate(dus, axis=1), w_in, w_out

        def second(s, fresh, act, du, w_in, w_out):
            y_part, dr_part = dot_nn(act, w_out), dot_nt(du, w_in)
            y_acc[...] = y_part if fresh else y_acc[...] + y_part
            dr_acc[...] = dr_part if fresh else dr_acc[...] + dr_part
            acc[s, 0] += dot_nn(x_turned, du)
            acc[s, 1] += dot_nn(dy_turned, act)

        order = (2, 3, 0, 1)
        kept = first(order[0])
        for i in range(1, 4):
            fresh = first(order[i])
            second(order[i - 1], i == 1, *kept)
            kept = fresh
        second(order[3], False, *kept)

        y = y_acc[...]
        dgate = jnp.sum(g.astype(F32) * y, axis=-1, keepdims=True)
        dr_low, y_low = dr_acc[...].astype(BF16), (gate * y).astype(BF16)
        for j, k in enumerate(names):
            x_all[k, 0:cap, :] = dr_low[j * cap : (j + 1) * cap, :]
            g_all[k] = y_low[j * cap : (j + 1) * cap, :]
            line = jnp.broadcast_to(dgate[j * cap : (j + 1) * cap, :], (cap, 128))
            if cap % 128:
                line = jnp.concatenate([line, jnp.zeros((128 - cap % 128, 128), F32)], axis=0)
            line = line.T[0:1, :]
            top = line.astype(BF16).astype(F32)
            middle = (line - top).astype(BF16).astype(F32)
            last = line - top - middle
            long = line.shape[1]
            meta = jnp.concatenate([top, middle, last, jnp.zeros((13, long), F32)], axis=0)
            meta = jnp.concatenate([meta, jnp.zeros((16, width - long), F32)], axis=1)
            x_all[k, cap : cap + 16, :] = meta.astype(BF16)

        for k in names:

            @pl.when(k > 0)
            def _(k=k):
                dr_copy(k).start()

            @pl.when(k == 0)
            def _():
                pltpu.make_async_copy(x_all.at[0], dr_ref.at[0], own_sem).start()

            y_copy(k).start()

        return 0

    lax.fori_loop(0, experts // group, one_tile, 0)

    pl.semaphore_signal(ready_sem, inc=1, device_id=sibling, device_id_type=MESH)
    for j in range(2):
        for side in range(2):
            w_all[j, side * width : (side + 1) * width, :] = acc[2 + j, side].astype(BF16)
    pl.semaphore_wait(ready_sem, 1)
    swaps = [
        pltpu.make_async_remote_copy(
            src_ref=w_all.at[j],
            dst_ref=w_all.at[2 + j],
            send_sem=pair_sem.at[j],
            recv_sem=pair_sem.at[2 + j],
            device_id=sibling,
            device_id_type=MESH,
        )
        for j in range(2)
    ]
    for copy in swaps:
        copy.start()
    results = []
    for j in range(2):
        swaps[j].wait()
        for side in range(2):
            at = slice(side * width, (side + 1) * width)
            w_all[2 + j, at, :] = (w_all[2 + j, at, :].astype(F32) + acc[j, side]).astype(BF16)
        for side, ref in enumerate(((in0_ref, out0_ref), (in1_ref, out1_ref))[j]):
            at = pl.ds(side * width, width)
            results.append(
                pltpu.make_async_copy(w_all.at[2 + j, at, :], ref, w_sem.at[2 * j + side])
            )
            results[-1].start()
    for copy in results:
        copy.wait()

    def settle(k, _):
        x_copy(k).wait_send()
        dr_copy(k).wait()
        y_copy(k).wait()
        return 0

    lax.fori_loop(1, experts, settle, 0)
    y_copy(0).wait()
    pltpu.make_async_copy(x_all.at[0], dr_ref.at[0], own_sem).wait()


def backward_kernel(
    tall_ref,
    gy_ref,
    x_ref,
    h_ref,
    qkv_ref,
    o_ref,
    p_ref,
    wall_ref,
    dr_ref,
    y_ref,
    grad_ref,
    all_ref,
    out_ref,
    small,
    acc,
    small_acc,
    dqkv,
    dp_all,
    y_in,
    send_sem,
    recv_sem,
    own_sem,
    *,
    experts,
    cap,
):
    width = x_ref.shape[2]
    part, half, low = where_am_i(experts)
    step = pl.program_id(0)

    def swap_copy(k):
        return pltpu.make_async_remote_copy(
            src_ref=y_ref.at[k],
            dst_ref=y_in.at[k],
            send_sem=send_sem.at[k],
            recv_sem=recv_sem.at[k],
            device_id=partner(experts, part, half, low, k),
            device_id_type=MESH,
        )

    own_copy = pltpu.make_async_copy(y_ref.at[0], y_in.at[0], own_sem)

    @pl.when(step == 0)
    def _():
        greet([partner(experts, part, half, low, k) for k in range(1, experts)])
        for k in range(experts - 1, 0, -1):
            swap_copy(k).start()
        own_copy.start()
        small[...] = wall_ref[0, :, 2 * width :].astype(F32).T
        acc[...] = jnp.zeros_like(acc)
        small_acc[...] = jnp.zeros_like(small_acc)

    gy = gy_ref[0].astype(F32)
    h = h_ref[step]
    unit, spread = norm_parts(h)
    gain, shift = small[experts + 2 : experts + 3, :], small[experts + 3 : experts + 4, :]
    n2 = (unit * gain + shift).astype(BF16)
    slot = lax.broadcasted_iota(jnp.int32, (PAD, cap), 1)

    def owners(image, k):
        first = tall_ref[image, :, 0:1] - k * cap
        second = tall_ref[image, :, 1:2] - k * cap
        return ((first == slot) | (second == slot)).astype(F32).astype(BF16)

    dn2 = jnp.zeros((PAD, width), F32)
    for k in range(experts):
        pick = owners(step, k)
        dn2 = dn2 + dot_nn(pick, dr_ref[k, 0:cap, :])
        line = dot_nt(dr_ref[k, cap : cap + 16, 0:cap], pick)
        dp_all[pl.ds(flipped(experts, part, k), 1), :] = (
            line[0:1, :] + line[1:2, :] + line[2:3, :]
        )
    probs = p_ref[0]
    dp = dp_all[...]
    dlogits = (probs * (dp - jnp.sum(dp * probs, axis=0, keepdims=True))).astype(BF16)
    small_acc[0:experts, :] += dot_nn(dlogits, n2)
    dn2 = dn2 + dot_tn(dlogits, small[0:experts, :].astype(BF16))
    small_acc[experts + 2 : experts + 3, :] += jnp.sum(dn2 * unit, axis=0, keepdims=True)
    small_acc[experts + 3 : experts + 4, :] += jnp.sum(dn2, axis=0, keepdims=True)
    dh = gy + norm_back(dn2, unit, spread, gain)
    dh_low = dh.astype(BF16)
    acc[:, 3 * width :] += dot_tn(o_ref[0], dh_low)
    do = dot_nt(dh_low, wall_ref[1, :, width : 2 * width]).astype(BF16)

    lane = lax.broadcasted_iota(jnp.int32, (PAD, 128), 1)
    key_at = lax.broadcasted_iota(jnp.int32, (PAD, PAD), 0)
    for pair in range(width // 128):
        q = qkv_ref[0, :, pair * 128 : (pair + 1) * 128]
        k = qkv_ref[0, :, width + pair * 128 : width + (pair + 1) * 128]
        v = qkv_ref[0, :, 2 * width + pair * 128 : 2 * width + (pair + 1) * 128]
        dop = do[:, pair * 128 : (pair + 1) * 128]
        parts = []
        for side in range(2):
            mine = (lane < HD) if side == 0 else (lane >= HD)
            k_mine = jnp.where(mine, k, jnp.zeros_like(k))
            v_mine = jnp.where(mine, v, jnp.zeros_like(v))
            scores = dot_nt(k_mine, q) * (HD**-0.5)
            scores = jnp.where(key_at < SEQ, scores, -1e30)
            expo = jnp.exp(scores - jnp.max(scores, axis=0, keepdims=True))
            prob = expo / jnp.sum(expo, axis=0, keepdims=True)
            dprob = dot_nt(v_mine, dop)
            dscore = prob * (dprob - jnp.sum(dprob * prob, axis=0, keepdims=True))
            dz = (dscore * (HD**-0.5)).astype(BF16)
            parts.append((dot_tn(dz, k), dot_nn(dz, q), dot_nn(prob.astype(BF16), dop)))
        for j in range(3):
            dqkv[:, j * width + pair * 128 : j * width + (pair + 1) * 128] = jnp.where(
                lane < HD, parts[0][j], parts[1][j]
            ).astype(BF16)

    unit, spread = norm_parts(x_ref[0].astype(F32))
    gain, shift = small[experts : experts + 1, :], small[experts + 1 : experts + 2, :]
    n1 = (unit * gain + shift).astype(BF16)
    dn1 = jnp.zeros((PAD, width), F32)
    for j in range(3):
        cols = slice(j * width, (j + 1) * width)
        acc[:, cols] += dot_tn(n1, dqkv[:, cols])
        dn1 = dn1 + dot_nt(
            dqkv[:, cols], wall_ref[j // 2, :, (j % 2) * width : (j % 2 + 1) * width]
        )
    small_acc[experts : experts + 1, :] += jnp.sum(dn1 * unit, axis=0, keepdims=True)
    small_acc[experts + 1 : experts + 2, :] += jnp.sum(dn1, axis=0, keepdims=True)
    grad_ref[0] = dh + norm_back(dn1, unit, spread, gain)

    @pl.when(step == pl.num_programs(0) - 1)
    def _():
        for j in range(4):
            all_ref[j // 2, :, (j % 2) * width : (j % 2 + 1) * width] = acc[
                :, j * width : (j + 1) * width
            ].astype(BF16)
        all_ref[0, :, 2 * width :] = small_acc[...].T.astype(BF16)
        all_ref[1, :, 2 * width :] = jnp.zeros((width, 128), BF16)
        for k in range(1, experts):
            swap_copy(k).wait()
        own_copy.wait()

        def one_image(image, _):
            total = h_ref[image]
            for k in range(experts):
                total = total + dot_nn(owners(image, k), y_in[k])
            out_ref[image] = total.astype(BF16)
            return 0

        lax.fori_loop(0, out_ref.shape[0], one_image, 0)


def adam_kernel(m_ref, f_ref, q_ref, a_ref, b_ref, w_out, f_out, q_out, c_out, *, rate, turn):
    grad = a_ref[...].astype(F32) + b_ref[...].astype(F32)
    if turn:
        grad = grad.T
    new = adam_step(m_ref[...], f_ref[...], q_ref[...], grad, rate)
    w_out[...], f_out[...], q_out[...], c_out[...] = new


def expert_adam(master, first_state, square, grads, rate, turn):
    shape = master.shape
    rows, cols = shape[1], shape[2]
    block = 128
    here = pl.BlockSpec((block, cols), lambda i: (i, 0))
    there = pl.BlockSpec((cols, block), lambda i: (0, i)) if turn else here
    new = pl.pallas_call(
        functools.partial(adam_kernel, rate=rate, turn=turn),
        grid=(rows // block,),
        out_shape=[jax.ShapeDtypeStruct((rows, cols), t) for t in (F32, F32, F32, BF16)],
        in_specs=[here, here, here, there, there],
        out_specs=[here] * 4,
        compiler_params=params(),
        cost_estimate=cost(9),
        name="adam",
    )(*(v.reshape(rows, cols) for v in (master, first_state, square)), *grads)
    return tuple(v.reshape(shape) for v in new)


def on_device(
    expert_axis,
    block_input,
    output_grad,
    routes,
    qkv_master,
    qkv_mean,
    qkv_square,
    proj_master,
    proj_mean,
    proj_square,
    router_master,
    router_mean,
    router_square,
    norm_master,
    norm_mean,
    norm_square,
    inner_master,
    inner_mean,
    inner_square,
    outer_master,
    outer_mean,
    outer_square,
):
    row_count, width = block_input.shape
    heads = width // HD
    images = row_count // SEQ
    tokens = images * PAD
    experts = router_master.shape[1]
    own_rows = qkv_master.shape[0]
    bound = row_count * 16 // (5 * experts) + 1
    cap = -(-bound // 16) * 16
    group = max(1, min(experts, 640 // cap // 2 * 2))
    while experts % group:
        group = group - 1
    slice_width = inner_master.shape[2]
    vmem = pl.BlockSpec(memory_space=pltpu.VMEM)
    smem = pl.BlockSpec(memory_space=pltpu.SMEM)
    anywhere = pl.BlockSpec(memory_space=pl.ANY)
    struct = jax.ShapeDtypeStruct

    ids = where_am_i(experts)[0].reshape(1).astype(jnp.int32)

    qkv_own = qkv_master.reshape(own_rows, heads, 3, HD).transpose(0, 2, 1, 3)
    qkv_own = qkv_own.reshape(own_rows, 3 * width)
    wall_own = jnp.concatenate(
        [
            qkv_own[:, : 2 * width],
            router_master,
            norm_master.T,
            jnp.zeros((own_rows, 128 - experts - 4), F32),
            qkv_own[:, 2 * width :],
            proj_master,
            jnp.zeros((own_rows, 128), F32),
        ],
        axis=1,
    )
    half_width = 2 * width + 128
    count = (width // own_rows).bit_length() - 2
    block = (2,) * count + (2 * own_rows, half_width)
    in_kernel = own_rows % 8 == 0

    both = jnp.concatenate([inner_master[0].astype(BF16), outer_master[0].astype(BF16)], axis=0)
    w_own = [lax.ppermute(both, AXES, weight_perm(experts, k)) for k in range(2)]

    def padded(values):
        return jnp.pad(values.reshape(images, SEQ, -1), ((0, 0), (0, PAD - SEQ), (0, 0)))

    tall = jnp.pad(
        routes.reshape(images, SEQ, 2), ((0, 0), (0, PAD - SEQ), (0, 0)), constant_values=-1
    ).reshape(tokens, 2)
    wide_slots, tall_slots = pl.pallas_call(
        functools.partial(routing_kernel, experts=experts, cap=cap),
        out_shape=(struct((2, tokens), jnp.int32), struct((tokens, 2), jnp.int32)),
        in_specs=[smem, vmem, vmem],
        out_specs=(vmem, vmem),
        compiler_params=params(),
        name="routing",
    )(ids, tall.T, tall)
    tall_slots = tall_slots.reshape(images, PAD, 2)

    gy = padded(output_grad)
    dma = pltpu.SemaphoreType.DMA
    wall = pl.pallas_call(
        gather_kernel,
        out_shape=struct((2,) + block, BF16),
        in_specs=[vmem],
        out_specs=anywhere,
        scratch_shapes=[
            pltpu.VMEM(wall_own.shape, F32),
            pltpu.VMEM((2,) + block, BF16),
            dma((2,)),
        ]
        + [dma((2, count))] * 4
        + [dma],
        compiler_params=params(collective_id=0, has_side_effects=True),
        cost_estimate=cost(50),
        name="gather_shared",
    )(wall_own)
    wall = wall.reshape(2, width, half_width)

    x = padded(block_input)

    def image_spec(*dims):
        return pl.BlockSpec((1,) + dims, lambda i: (i,) + (0,) * len(dims))

    def whole_spec(*dims, once=True):
        mode = dict(pipeline_mode=pl.Buffered(1)) if once else {}
        return pl.BlockSpec(dims, lambda i: (0,) * len(dims), **mode)

    qkv, attended, middle, second, probs, g_blocks = pl.pallas_call(
        functools.partial(forward_kernel, experts=experts, cap=cap),
        grid=(images,),
        out_shape=(
            struct((images, PAD, 3 * width), BF16),
            struct((images, PAD, width), BF16),
            struct((images, PAD, width), F32),
            struct((images, PAD, width), BF16),
            struct((images, experts, PAD), F32),
            struct((experts, cap, width), BF16),
        ),
        in_specs=[
            image_spec(PAD, width),
            whole_spec(2, width, half_width),
            whole_spec(2, tokens),
            whole_spec(tokens, width),
        ],
        out_specs=(
            image_spec(PAD, 3 * width),
            image_spec(PAD, width),
            image_spec(PAD, width),
            image_spec(PAD, width),
            image_spec(experts, PAD),
            anywhere,
        ),
        scratch_shapes=[
            pltpu.VMEM((128, width), F32),
            pltpu.VMEM((experts, cap, width), BF16),
            dma((experts,)),
            dma((experts,)),
            dma,
        ],
        compiler_params=params(collective_id=3, has_side_effects=True),
        cost_estimate=cost(50),
        name="forward",
    )(x, wall, wide_slots, gy.reshape(tokens, width))

    w_own_late, second = lax.optimization_barrier((w_own, second))
    w_sib = [lax.ppermute(w, AXES, core_perm(experts)) for w in w_own_late]
    router_low = wall[0, :, 2 * width : 2 * width + experts].T
    y_blocks, dr_blocks, in0, out0, in1, out1 = pl.pallas_call(
        functools.partial(expert_kernel, experts=experts, cap=cap, group=group),
        out_shape=(
            struct((experts, cap, width), BF16),
            struct((experts, cap + 16, width), BF16),
        )
        + (struct((width, slice_width), BF16),) * 4,
        in_specs=[vmem, vmem] + [anywhere] * 5 + [vmem],
        out_specs=[anywhere] * 6,
        scratch_shapes=[
            pltpu.VMEM((experts, cap + 16, width), BF16),
            pltpu.VMEM((experts, cap, width), BF16),
            pltpu.VMEM((experts, cap, width), BF16),
            pltpu.VMEM((4, 2 * width, slice_width), BF16),
            pltpu.VMEM((4, 2, width, slice_width), F32),
            pltpu.VMEM((group * cap, width), F32),
            pltpu.VMEM((group * cap, width), F32),
        ]
        + [dma((experts,))] * 5
        + [dma, dma((4,)), dma, dma((4,)), pltpu.SemaphoreType.REGULAR],
        compiler_params=params(collective_id=1, has_side_effects=True),
        cost_estimate=cost(140),
        name="experts",
    )(wide_slots, second.reshape(tokens, width), g_blocks, *w_own_late, *w_sib, router_low)

    grad_back = [
        [lax.ppermute(g, AXES, turned(weight_perm(experts, k))) for k, g in enumerate(pair)]
        for pair in ((in0, in1), (out0, out1))
    ]

    input_grad, shared_grad, block_output = pl.pallas_call(
        functools.partial(backward_kernel, experts=experts, cap=cap),
        grid=(images,),
        out_shape=(
            struct((images, PAD, width), F32),
            struct((2, width, half_width), BF16),
            struct((images, PAD, width), BF16),
        ),
        in_specs=[
            whole_spec(images, PAD, 2),
            image_spec(PAD, width),
            image_spec(PAD, width),
            whole_spec(images, PAD, width),
            image_spec(PAD, 3 * width),
            image_spec(PAD, width),
            image_spec(experts, PAD),
            whole_spec(2, width, half_width),
            whole_spec(experts, cap + 16, width),
            anywhere,
        ],
        out_specs=(
            image_spec(PAD, width),
            whole_spec(2, width, half_width, once=False),
            whole_spec(images, PAD, width, once=False),
        ),
        scratch_shapes=[
            pltpu.VMEM((128, width), F32),
            pltpu.VMEM((width, 4 * width), F32),
            pltpu.VMEM((128, width), F32),
            pltpu.VMEM((PAD, 3 * width), BF16),
            pltpu.VMEM((experts, PAD), F32),
            pltpu.VMEM((experts, cap, width), BF16),
            dma((experts,)),
            dma((experts,)),
            dma,
        ],
        compiler_params=params(collective_id=4, has_side_effects=True),
        cost_estimate=cost(60),
        name="backward",
    )(tall_slots, gy, x, middle, qkv, attended, probs, wall, dr_blocks, y_blocks)
    input_grad = input_grad[:, :SEQ].reshape(row_count, width)
    block_output = block_output[:, :SEQ].reshape(row_count, width)

    landings = [
        pltpu.VMEM((2,) * (count - 1 - i) + (2 * own_rows, c.stop - c.start), BF16)
        for c in parts_of(half_width)
        for i in range(count)
    ]
    shared_own = pl.pallas_call(
        reduce_kernel,
        out_shape=struct((own_rows, 2 * half_width), F32),
        in_specs=[vmem],
        out_specs=vmem,
        scratch_shapes=[
            pltpu.VMEM(block, BF16),
            pltpu.VMEM(block, BF16),
            pltpu.VMEM((2 * own_rows, half_width), F32),
            pltpu.VMEM((2, own_rows, half_width), F32),
            dma((4,)),
            dma((2, count)),
            dma((2, count)),
            dma((2,)),
        ]
        + landings,
        compiler_params=params(collective_id=2, has_side_effects=True),
        cost_estimate=cost(50),
        name="reduce_shared",
    )(shared_grad.reshape((2,) + block))
    qkv_owned = jnp.concatenate(
        [shared_own[:, : 2 * width], shared_own[:, half_width : half_width + width]], axis=1
    )
    qkv_owned = qkv_owned.reshape(own_rows, 3, heads, HD).transpose(0, 2, 1, 3)
    qkv_owned = qkv_owned.reshape(own_rows, 3 * width)
    proj_owned = shared_own[:, half_width + width : half_width + 2 * width]
    router_owned = shared_own[:, 2 * width : 2 * width + experts]
    norm_owned = shared_own[:, 2 * width + experts : 2 * width + experts + 4].T

    qkv_new = adam_step(qkv_master, qkv_mean, qkv_square, qkv_owned, 2.0 * width ** (-0.5))
    proj_new = adam_step(
        proj_master, proj_mean, proj_square, proj_owned, 2.0 * (width // 16) ** (-0.5)
    )
    router_new = adam_step(
        router_master, router_mean, router_square, router_owned, 2.0 * (4 * width) ** (-0.5)
    )
    norm_new = adam_step(norm_master, norm_mean, norm_square, norm_owned, NORM_RATE)
    inner_new = expert_adam(
        inner_master, inner_mean, inner_square, grad_back[0], 2.0 * width ** (-0.5), False
    )
    outer_new = expert_adam(
        outer_master,
        outer_mean,
        outer_square,
        grad_back[1],
        2.0 * max(1, FF * 4 // (experts * experts)) ** (-0.5),
        True,
    )
    return (
        block_output,
        input_grad,
        *qkv_new,
        *proj_new,
        *router_new,
        *norm_new,
        *inner_new,
        *outer_new,
    )


def solution(mesh):
    rows = P(AXES, None)
    cols = P(None, AXES)
    inner = P("expert", None, "head")
    outer = P("expert", "head", None)
    in_specs = (rows,) * 12 + (cols,) * 3 + (inner,) * 3 + (outer,) * 3
    out_specs = (rows,) * 14 + (cols,) * 4 + (inner,) * 4 + (outer,) * 4
    return jax.shard_map(
        functools.partial(on_device, mesh.shape["expert"]),
        mesh=mesh,
        in_specs=in_specs,
        out_specs=out_specs,
        check_vma=False,
    )
```

time: 1580 us -> 612 us (0.39)
  waiting for transfers between devices: 552 us -> 69.6 us
  Pallas kernels: 0 us -> 454 us
  blocking collectives: 379 us -> 0 us
  local copies, waits for them, and re-layouts: 294 us -> 25.7 us
  matrix products: 246 us -> 0 us
  other arithmetic: 76.1 us -> 8.34 us
  starting transfers between devices: 11.4 us -> 40.7 us
    pallas_call x0 -> x8, Pallas kernels: none -> 454 us  [the longest x1 133 us: on_device(): pl.pallas_call(functools.partial(expert_kernel, experts=experts, cap=cap,...]
    reduce_scatter x4 -> x0, waiting for transfers between devices: 266 us -> none  [the longest x1 120 us: on_device(): lax.psum_scatter(partial_value.astype(jnp.bfloat16), 'head', scatter_dime...]
    dot_general x21 -> x0, matrix products: 246 us -> none  [the longest x1 35.1 us: on_device(): jnp.einsum('rd,fd->rf', gathered_grads, outer_low, preferred_element_type...]
    all_gather x4 -> x0, waiting for transfers between devices: 199 us -> none  [the longest x1 97.1 us: on_device(): lax.all_gather(owner_grads, 'head', axis=0, tiled=True)]
    all_to_all x2 -> x0, blocking collectives: 196 us -> none  [the longest x1 104 us: on_device(): lax.all_to_all(slot_grads.reshape(expert_count, capacity, model_width), '...]
    all_gather x2 -> x0, blocking collectives: 143 us -> none  [the longest x1 99.8 us: on_device(): lax.all_gather(router_master.astype(jnp.bfloat16), ('expert', 'head'), ax...]
    all_to_all x2 -> x0, waiting for transfers between devices: 87.5 us -> none  [the longest x1 87.5 us: on_device(): lax.all_to_all(row_grads, 'expert', split_axis=0, concat_axis=0, tiled=True)]
    reshape x13 -> x10, local copies, waits for them, and re-layouts: 78.1 us -> 7.5 us  [the longest x2 3.21 us: padded(): values.reshape(images, SEQ, -1)]
  transfers between devices with their start and end apart: 10 -> 8, of which waited for: 7 -> 4; matrix products, arithmetic and copies ran while one was open for 17% -> 4% of each run, Pallas kernels for 0% -> 33%
where the time goes in v1:
time: 612 us; the launch traced here: 600 us
  Pallas kernels  454 us (74%)
  waiting for transfers between devices  69.6 us (11%)
  starting transfers between devices  40.7 us (7%)
  local copies, waits for them, and re-layouts  25.7 us (4%)
  other arithmetic  8.34 us (1%)
    pallas_call x1, Pallas kernels, on_device(): pl.pallas_call(functools.partial(expert_kernel, experts=experts, cap=cap,...  133 us
    pallas_call x1, Pallas kernels, on_device(): pl.pallas_call(gather_kernel, out_shape=struct((2,) + block, BF16), in_sp...  118 us
    pallas_call x1, Pallas kernels, on_device(): pl.pallas_call(functools.partial(backward_kernel, experts=experts, cap=ca...  68.6 us
    pallas_call x1, Pallas kernels, on_device(): pl.pallas_call(functools.partial(forward_kernel, experts=experts, cap=cap...  68.1 us
    ppermute x4, waiting for transfers between devices, on_device(): lax.ppermute(g, AXES, turned(weight_perm(experts, k)))  67 us
    pallas_call x1, Pallas kernels, on_device(): pl.pallas_call(reduce_kernel, out_shape=struct((own_rows, 2 * half_width)...  47.2 us
    ppermute x4, starting transfers between devices, on_device(): lax.ppermute(g, AXES, turned(weight_perm(experts, k)))  20.8 us
    ppermute x2, starting transfers between devices, on_device(): lax.ppermute(both, AXES, weight_perm(experts, k))  19.3 us
  transfers between devices with their start and end apart: 8, of which 4 were waited for; matrix products, arithmetic and copies ran while one was open for 4% of the time, Pallas kernels for 33%

profile of v1, /device:TPU:0, one launch (start us, length us, event | category | flops | bytes accessed | tf_op | source)
XLA Modules:
  0.0 600.1 jit_solution(17382771915793407032)
XLA Ops:
  0.7 2.6 bitcast_convert_fusion
  3.3 0.0 copy-start.2
  3.3 1.6 pad_maximum_fusion
  4.9 19.3 %collective-permute-start = (bf16[1536,768]{1,0:T(8,128)(2,1)}, bf16[1536,768]{1,0:T(8,128)(2,1)}, u32[]{:S(2)}, u32[]{:S(2)}) collective-permute-start(bf16[1536,768]{1,0:T(8,128)(2,1)} %pad_maximum_fusion), channel_id=1, source_target_pairs={{0,0},{1,1},{2,18},{3,19},{4,4},{5,5},{6,22},{7,23},{8,2},{9,3},{1... | collective-permute-start | bytes 7077896 | tf_op jit(solution)/shard_map/ppermute | solution.py:933
  24.2 0.3 reshape.144
  24.5 0.1 copy.101
  24.6 0.1 reshape.145
  24.7 0.0 copy-start.4
  24.8 0.1 reshape.139
  24.9 0.2 copy.99
  25.1 0.0 copy-start
  25.1 0.8 copy.100.wide_ref
  25.9 1.6 reshape.142
  27.5 1.6 reshape.143
  29.1 0.0 copy-start.20
  29.2 1.1 pad.12.gy_ref
  30.3 1.1 pad.13.x_ref
  31.4 0.1 copy.103
  31.5 0.1 copy.102
  31.6 0.8 concatenate.9.own_ref
  32.4 117.5 %gather_shared.1 = bf16[2,2,2,2,2,48,1664]{6,5,4,3,2,1,0:T(8,128)(2,1)} custom-call(f32[24,3328]{1,0:T(8,128)} %concatenate.9.own_ref), custom_call_target="tpu_custom_call" | custom-call | flops 54999998464 | bytes 150000000 | tf_op jit(solution)/shard_map/gather_shared/pallas_call | solution.py:953
  150.0 2.7 routing.1
  152.8 68.1 %forward.1 = (bf16[4,208,2304]{2,1,0:T(8,128)(2,1)}, bf16[4,208,768]{2,1,0:T(8,128)(2,1)}, f32[4,208,768]{2,1,0:T(8,128)}, bf16[4,208,768]{2,1,0:T(8,128)(2,1)},...) custom-call(bf16[4,208,768]{2,1,0:T(8,128)(2,1)} %pad.13.x_ref, bf16[2,768,1664]{2,1,0:T(8,128)(2,1)} %bitcast.47, ...), custom_call_target="tpu_custom_call" | custom-call | flops 54999998464 | bytes 150000000 | tf_op jit(solution)/shard_map/forward/pallas_call | solution.py:980
  220.9 0.1 collective-permute-start.2
  220.9 0.5 collective-permute-start.3
  221.4 0.9 slice_bitcast_fusion
  222.4 0.7 copy.104.router_ref
  223.1 0.7 copy.106
  223.8 0.7 copy.109
  224.5 0.7 copy.116
  225.1 0.7 copy.114
  225.8 0.7 copy.115
  226.5 1.7 collective-permute-done.2.w2_ref
  228.3 0.9 collective-permute-done.3.w3_ref
  229.2 0.5 copy-done.27
  229.7 132.8 %experts.1 = (bf16[8,320,768]{2,1,0:T(8,128)(2,1)}, bf16[8,336,768]{2,1,0:T(8,128)(2,1)}, bf16[768,768]{1,0:T(8,128)(2,1)}, bf16[768,768]{1,0:T(8,128)(2,1)}, bf...) custom-call(s32[2,832]{1,0:T(2,128)} %get-tuple-element.55.wide_ref, bf16[832,768]{1,0:T(8,128)(2,1)} %bitcast.62, ...), custom_call_target="tpu_custom_call" | custom-call | flops 153999998976 | bytes 420000000 | tf_op jit(solution)/shard_map/experts/pallas_call | solution.py:1020
  362.5 68.6 %backward.1 = (f32[4,208,768]{2,1,0:T(8,128)}, bf16[2,768,1664]{2,1,0:T(8,128)(2,1)}, bf16[4,208,768]{2,1,0:T(8,128)(2,1)}) custom-call(s32[4,208,2]{2,1,0:T(8,128)} %bitcast.54, bf16[4,208,768]{2,1,0:T(8,128)(2,1)} %pad.12.gy_ref, bf16[4,208,768]{2,1,0:T(8,128)(2,1)} %pad.13.x_ref, f32[4,208,768]{2,1,0:T(8,128)} %get-tuple-element.56.h_ref, ...), custom_call_target="tpu_custom_call" | custom-call | flops 65999998976 | bytes 180000000 | tf_op jit(solution)/shard_map/backward/pallas_call | solution.py:1050
  431.1 47.2 %reduce_shared.1 = f32[24,3328]{1,0:T(8,128)} custom-call(bf16[2,2,2,2,2,48,1664]{6,5,4,3,2,1,0:T(8,128)(2,1)} %bitcast.55), custom_call_target="tpu_custom_call" | custom-call | flops 54999998464 | bytes 150000000 | tf_op jit(solution)/shard_map/reduce_shared/pallas_call | solution.py:1098
  478.4 1.0 slice.35
  479.4 1.6 fusion.8
  481.1 0.1 reshape.152
  481.2 0.2 copy.105
  481.4 0.4 reshape.153
  481.8 10.4 %collective-permute-start.4 = (bf16[768,768]{1,0:T(8,128)(2,1)}, bf16[768,768]{1,0:T(8,128)(2,1)}, u32[]{:S(2)}, u32[]{:S(2)}) collective-permute-start(bf16[768,768]{1,0:T(8,128)(2,1)} %get-tuple-element.70), channel_id=1, source_target_pairs={{0,0},{1,1},{18,2},{19,3},{4,4},{5,5},{22,6},{23,7},{2,8},{3,9},{1... | collective-permute-start | bytes 3538952 | tf_op jit(solution)/shard_map/ppermute | solution.py:1046
  492.2 10.4 %collective-permute-start.6 = (bf16[768,768]{1,0:T(8,128)(2,1)}, bf16[768,768]{1,0:T(8,128)(2,1)}, u32[]{:S(2)}, u32[]{:S(2)}) collective-permute-start(bf16[768,768]{1,0:T(8,128)(2,1)} %get-tuple-element.76), channel_id=1, source_target_pairs={{0,0},{1,1},{18,2},{19,3},{4,4},{5,5},{22,6},{23,7},{2,8},{3,9},{1... | collective-permute-start | bytes 3538952 | tf_op jit(solution)/shard_map/ppermute | solution.py:1046
  502.7 1.0 fusion.10
  503.6 0.7 fusion.6
  504.4 0.1 slice.33
  504.5 1.3 reshape.149
  505.8 1.9 slice.34
  507.7 1.7 reshape.150
  509.4 0.7 copy.118
  510.1 0.7 copy.119
  510.8 0.7 copy.120
  511.4 0.7 copy.121
  512.1 0.8 fusion.4
  512.9 0.7 copy.122
  513.5 0.7 copy.123
  514.2 0.7 copy.124
  514.9 0.6 copy.125
  515.5 25.4 %collective-permute-done.5.b_ref = bf16[768,768]{1,0:T(8,128)(2,1)} collective-permute-done((bf16[768,768]{1,0:T(8,128)(2,1)}, bf16[768,768]{1,0:T(8,128)(2,1)}, u32[]{:S(2)}, u32[]{:S(2)}) %collective-permute-start.5) | collective-permute-done | bytes 1179680 | tf_op jit(solution)/shard_map/ppermute | solution.py:1046
  540.9 8.7 %adam.2 = (f32[768,768]{1,0:T(8,128)}, f32[768,768]{1,0:T(8,128)}, f32[768,768]{1,0:T(8,128)}, bf16[768,768]{1,0:T(8,128)(2,1)}) custom-call(f32[768,768]{1,0:T(8,128)} %bitcast.41, f32[768,768]{1,0:T(8,128)} %bitcast.50, f32[768,768]{1,0:T(8,128)} %bitcast.51, bf16[768,768]{1,0:T(8,128)(2,1)} %collective-permute-done.4.a_ref, ...), custom_call_target="tpu_custom_call" | custom-call | flops 9900000256 | bytes 27000000 | tf_op jit(solution)/shard_map/adam/pallas_call | solution.py:857
  549.6 41.5 %collective-permute-done.7.b_ref = bf16[768,768]{1,0:T(8,128)(2,1)} collective-permute-done((bf16[768,768]{1,0:T(8,128)(2,1)}, bf16[768,768]{1,0:T(8,128)(2,1)}, u32[]{:S(2)}, u32[]{:S(2)}) %collective-permute-start.7) | collective-permute-done | bytes 1179680 | tf_op jit(solution)/shard_map/ppermute | solution.py:1046
  591.2 8.8 %adam.3 = (f32[768,768]{1,0:T(8,128)}, f32[768,768]{1,0:T(8,128)}, f32[768,768]{1,0:T(8,128)}, bf16[768,768]{1,0:T(8,128)(2,1)}) custom-call(f32[768,768]{1,0:T(8,128)} %bitcast.42, f32[768,768]{1,0:T(8,128)} %bitcast.52, f32[768,768]{1,0:T(8,128)} %bitcast.53, bf16[768,768]{1,0:T(8,128)(2,1)} %collective-permute-done.6.a_ref, ...), custom_call_target="tpu_custom_call" | custom-call | flops 9900000256 | bytes 27000000 | tf_op jit(solution)/shard_map/adam/pallas_call | solution.py:857
  (69 shorter events, 0.2 us)
Async XLA Ops:
  3.3 20.9 %copy-start.2 = (f32[24,2304]{1,0:T(8,128)S(1)}, f32[24,2304]{1,0:T(8,128)}, u32[]{:S(2)}) copy-start(f32[24,2304]{1,0:T(8,128)} %param.24) | copy-start | bytes 663556
  4.9 19.9 %copy-start.21 = (s32[788,2]{0,1:T(2,128)S(1)}, s32[788,2]{0,1:T(2,128)}, u32[]{:S(2)}) copy-start(s32[788,2]{0,1:T(2,128)} %param.23) | copy-start | bytes 18916
  4.9 216.0 %collective-permute-start = (bf16[1536,768]{1,0:T(8,128)(2,1)}, bf16[1536,768]{1,0:T(8,128)(2,1)}, u32[]{:S(2)}, u32[]{:S(2)}) collective-permute-start(bf16[1536,768]{1,0:T(8,128)(2,1)} %pad_maximum_fusion), channel_id=1, source_target_pairs={{0,0},{1,1},{2,18},{3,19},{4,4},{5,5},{6,22},{7,23},{8,2},{9,3},{1... | collective-permute-start | bytes 7077896 | tf_op jit(solution)/shard_map/ppermute | solution.py:933
  24.2 196.7 %collective-permute-start.1 = (bf16[1536,768]{1,0:T(8,128)(2,1)}, bf16[1536,768]{1,0:T(8,128)(2,1)}, u32[]{:S(2)}, u32[]{:S(2)}) collective-permute-start(bf16[1536,768]{1,0:T(8,128)(2,1)} %pad_maximum_fusion), channel_id=1, source_target_pairs={{0,18},{1,19},{2,0},{3,1},{4,22},{5,23},{6,4},{7,5},{8,16},{9,17},... | collective-permute-start | bytes 7077896 | tf_op jit(solution)/shard_map/ppermute | solution.py:933
  24.7 4.4 copy-start.4
  25.1 4.0 copy-start
  29.1 2.3 copy-start.22
  29.1 2.4 copy-start.20
  29.2 2.5 copy-start.5
  30.3 1.3 slice-start
  30.3 1.3 slice-start.1
  31.5 118.5 %copy-start.11 = (f32[24,8]{1,0:T(8,128)}, f32[24,8]{1,0:T(8,128)S(1)}, u32[]{:S(2)}) copy-start(f32[24,8]{1,0:T(8,128)S(1)} %copy.103) | copy-start | bytes 2308
  31.6 118.4 %copy-start.9 = (f32[4,24]{0,1:T(8,128)}, f32[4,24]{0,1:T(8,128)S(1)}, u32[]{:S(2)}) copy-start(f32[4,24]{0,1:T(8,128)S(1)} %copy.102) | copy-start | bytes 1156
  152.8 70.3 %copy-start.23 = (f32[24,8]{0,1:T(8,128)S(1)}, f32[24,8]{0,1:T(8,128)}, u32[]{:S(2)}) copy-start(f32[24,8]{0,1:T(8,128)} %param.31) | copy-start | bytes 2308
  152.8 71.0 %copy-start.24 = (f32[24,8]{0,1:T(8,128)S(1)}, f32[24,8]{0,1:T(8,128)}, u32[]{:S(2)}) copy-start(f32[24,8]{0,1:T(8,128)} %param.32) | copy-start | bytes 2308
  152.8 72.4 %copy-start.25 = (f32[4,24]{1,0:T(4,128)S(1)}, f32[4,24]{1,0:T(4,128)}, u32[]{:S(2)}) copy-start(f32[4,24]{1,0:T(4,128)} %param.34) | copy-start | bytes 1156
  152.8 73.1 %copy-start.26 = (f32[4,24]{1,0:T(4,128)S(1)}, f32[4,24]{1,0:T(4,128)}, u32[]{:S(2)}) copy-start(f32[4,24]{1,0:T(4,128)} %param.35) | copy-start | bytes 1156
  220.9 7.4 %collective-permute-start.2 = (bf16[1536,768]{1,0:T(8,128)(2,1)}, bf16[1536,768]{1,0:T(8,128)(2,1)S(1)}, u32[]{:S(2)}, u32[]{:S(2)}) collective-permute-start(bf16[1536,768]{1,0:T(8,128)(2,1)} %collective-permute-done.w0_ref), channel_id=1, source_target_pairs={{0,1},{1,0},{2,3},{3,2},{4,5},{5,4},{6,7},{7,6},{8,9},{9,8},{10,11... | collective-permute-start | bytes 7077896 | tf_op jit(solution)/shard_map/ppermute | solution.py:1018
  220.9 8.2 %collective-permute-start.3 = (bf16[1536,768]{1,0:T(8,128)(2,1)}, bf16[1536,768]{1,0:T(8,128)(2,1)}, u32[]{:S(2)}, u32[]{:S(2)}) collective-permute-start(bf16[1536,768]{1,0:T(8,128)(2,1)} %collective-permute-done.1.w1_ref), channel_id=1, source_target_pairs={{0,1},{1,0},{2,3},{3,2},{4,5},{5,4},{6,7},{7,6},{8,9},{9,8},{10,11... | collective-permute-start | bytes 7077896 | tf_op jit(solution)/shard_map/ppermute | solution.py:1018
  228.3 1.4 copy-start.27
  431.1 48.2 %copy-start.6 = (f32[24,768]{1,0:T(8,128)S(1)}, f32[24,768]{1,0:T(8,128)}, u32[]{:S(2)}) copy-start(f32[24,768]{1,0:T(8,128)} %param.27) | copy-start | bytes 221188
  431.1 48.2 %copy-start.13 = (f32[24,768]{1,0:T(8,128)S(1)}, f32[24,768]{1,0:T(8,128)}, u32[]{:S(2)}) copy-start(f32[24,768]{1,0:T(8,128)} %param.28) | copy-start | bytes 221188
  431.1 48.2 %copy-start.14 = (f32[24,768]{1,0:T(8,128)S(1)}, f32[24,768]{1,0:T(8,128)}, u32[]{:S(2)}) copy-start(f32[24,768]{1,0:T(8,128)} %param.29) | copy-start | bytes 221188
  478.3 24.3 %copy-start.3 = (f32[24,2304]{1,0:T(8,128)S(1)}, f32[24,2304]{1,0:T(8,128)}, u32[]{:S(2)}) copy-start(f32[24,2304]{1,0:T(8,128)} %param.24) | copy-start | bytes 663556
  478.3 24.3 %copy-start.7 = (f32[24,2304]{1,0:T(8,128)S(1)}, f32[24,2304]{1,0:T(8,128)}, u32[]{:S(2)}) copy-start(f32[24,2304]{1,0:T(8,128)} %param.25) | copy-start | bytes 663556
  478.4 24.3 %copy-start.8 = (f32[24,2304]{1,0:T(8,128)S(1)}, f32[24,2304]{1,0:T(8,128)}, u32[]{:S(2)}) copy-start(f32[24,2304]{1,0:T(8,128)} %param.26) | copy-start | bytes 663556
  481.0 22.6 %copy-start.12 = (f32[24,8]{1,0:T(8,128)S(1)}, f32[24,8]{1,0:T(8,128)}, u32[]{:S(2)}) copy-start(f32[24,8]{1,0:T(8,128)} %copy-done.11) | copy-start | bytes 2308
  481.0 22.6 %copy-start.18 = (f32[24,8]{1,0:T(8,128)S(1)}, f32[24,8]{1,0:T(8,128)}, u32[]{:S(2)}) copy-start(f32[24,8]{1,0:T(8,128)} %copy.106) | copy-start | bytes 2308
  481.0 22.6 %copy-start.19 = (f32[24,8]{1,0:T(8,128)S(1)}, f32[24,8]{1,0:T(8,128)}, u32[]{:S(2)}) copy-start(f32[24,8]{1,0:T(8,128)} %copy.109) | copy-start | bytes 2308
  481.1 23.3 %copy-start.1 = (bf16[4,208,768]{2,1,0:T(8,128)(2,1)S(1)}, bf16[4,208,768]{2,1,0:T(8,128)(2,1)}, u32[]{:S(2)}) copy-start(bf16[4,208,768]{2,1,0:T(8,128)(2,1)} %get-tuple-element.67) | copy-start | bytes 3833860
  481.8 33.7 %collective-permute-start.4 = (bf16[768,768]{1,0:T(8,128)(2,1)}, bf16[768,768]{1,0:T(8,128)(2,1)}, u32[]{:S(2)}, u32[]{:S(2)}) collective-permute-start(bf16[768,768]{1,0:T(8,128)(2,1)} %get-tuple-element.70), channel_id=1, source_target_pairs={{0,0},{1,1},{18,2},{19,3},{4,4},{5,5},{22,6},{23,7},{2,8},{3,9},{1... | collective-permute-start | bytes 3538952 | tf_op jit(solution)/shard_map/ppermute | solution.py:1046
  492.2 48.7 %collective-permute-start.5 = (bf16[768,768]{1,0:T(8,128)(2,1)}, bf16[768,768]{1,0:T(8,128)(2,1)}, u32[]{:S(2)}, u32[]{:S(2)}) collective-permute-start(bf16[768,768]{1,0:T(8,128)(2,1)} %get-tuple-element.71), channel_id=1, source_target_pairs={{18,0},{19,1},{0,2},{1,3},{22,4},{23,5},{4,6},{5,7},{16,8},{17,9},... | collective-permute-start | bytes 3538952 | tf_op jit(solution)/shard_map/ppermute | solution.py:1046
  492.2 57.4 %collective-permute-start.6 = (bf16[768,768]{1,0:T(8,128)(2,1)}, bf16[768,768]{1,0:T(8,128)(2,1)}, u32[]{:S(2)}, u32[]{:S(2)}) collective-permute-start(bf16[768,768]{1,0:T(8,128)(2,1)} %get-tuple-element.76), channel_id=1, source_target_pairs={{0,0},{1,1},{18,2},{19,3},{4,4},{5,5},{22,6},{23,7},{2,8},{3,9},{1... | collective-permute-start | bytes 3538952 | tf_op jit(solution)/shard_map/ppermute | solution.py:1046
  502.6 88.5 %collective-permute-start.7 = (bf16[768,768]{1,0:T(8,128)(2,1)}, bf16[768,768]{1,0:T(8,128)(2,1)}, u32[]{:S(2)}, u32[]{:S(2)}) collective-permute-start(bf16[768,768]{1,0:T(8,128)(2,1)} %get-tuple-element.77), channel_id=1, source_target_pairs={{18,0},{19,1},{0,2},{1,3},{22,4},{23,5},{4,6},{5,7},{16,8},{17,9},... | collective-permute-start | bytes 3538952 | tf_op jit(solution)/shard_map/ppermute | solution.py:1046
  507.7 4.4 copy-start.10
  507.7 4.4 copy-start.15
  507.7 4.4 copy-start.16
  507.7 4.4 copy-start.17

commit v2 on v1

--- a/solution.py
+++ b/solution.py
@@ -23,7 +23,7 @@
 AXES = ("expert", "head")
 F32 = jnp.float32
 BF16 = jnp.bfloat16
-VMEM_BYTES = 60 * 2**20
+VMEM_BYTES = 62 * 2**20
 MESH = pl.DeviceIdType.MESH
 
 
@@ -58,40 +58,8 @@
     return pltpu.CompilerParams(vmem_limit_bytes=VMEM_BYTES, **kw)
 
 
-def spot_of(expert_axis, half, part, low):
-    quarter = expert_axis // 4
-    a, b, c = part // (2 * quarter), (part // quarter) % 2, part % quarter
-    return (half * (expert_axis // 2) + a * quarter + c) * 4 + ((a + b + half) % 2) * 2 + low
-
-
-def row_perm(expert_axis, k):
-    return [
-        (spot_of(expert_axis, r, f, lo), spot_of(expert_axis, r, f ^ k, lo))
-        for r in range(2)
-        for lo in range(2)
-        for f in range(expert_axis)
-    ]
-
-
-def weight_perm(expert_axis, k):
-    return [
-        (f * 4 + h, spot_of(expert_axis, (h // 2) ^ k, f, h % 2))
-        for f in range(expert_axis)
-        for h in range(4)
-    ]
-
-
-def turned(perm):
-    return [(b, a) for a, b in perm]
-
-
-def core_perm(expert_axis):
-    return [(d, d ^ 1) for d in range(expert_axis * 4)]
-
-
-def routing_kernel(ids_ref, wide_ref, tall_ref, wide_out, tall_out, *, experts, cap):
+def route(part, wide_ref, tall_ref, wide_out, tall_out, experts, cap):
     tokens = wide_ref.shape[1]
-    part = ids_ref[0]
     row = lax.broadcasted_iota(jnp.int32, (tokens, tokens), 0)
     col = lax.broadcasted_iota(jnp.int32, (tokens, tokens), 1)
 
@@ -121,7 +89,15 @@
         ],
         axis=1,
     ).astype(jnp.int32)
-    tall_out[...] = jnp.where(tall_ref[...] < 0, -1, tall * cap + place)
+    tall_out[...] = jnp.where(tall_ref[...] < 0, -1, tall * cap + place).reshape(tall_out.shape)
+
+
+def spread_images(stage, rows, out_ref):
+    stage[0 : rows.shape[0], :] = rows.astype(F32)
+    at = lax.broadcasted_iota(jnp.int32, (PAD, 1), 0)
+    for i in range(out_ref.shape[0]):
+        image = stage[i * SEQ : i * SEQ + PAD, :]
+        out_ref[i] = jnp.where(at < SEQ, image, 0.0).astype(BF16)
 
 
 def where_am_i(experts):
@@ -150,13 +126,24 @@
     return (row, lax.rem(lax.div(there, quarter) + a + half, 2) * 2 + low)
 
 
+def sequence(experts):
+    far = experts // 2
+    return [0] + list(range(far, experts)) + list(range(far - 1, 0, -1))
+
+
 def block_at(experts, j):
-    far = experts // 2
-    if isinstance(j, int):
-        return far if j == 0 else 0 if j == 1 else j + far - 1 if j <= far else j - far
-    return jnp.where(
-        j == 0, far, jnp.where(j == 1, 0, jnp.where(j <= far, j + far - 1, j - far))
-    )
+    block = jnp.int32(0)
+    for i, k in enumerate(sequence(experts)):
+        block = jnp.where(j == i, k, block)
+    return block
+
+
+def early_parts(experts):
+    turns = sequence(experts)
+    last = turns[experts // 2]
+    first = [k for k in turns[experts // 2 - 1 :] if k != last]
+    rest = [k for k in turns if k and k != last and k not in first]
+    return first, rest[::-1], [last], []
 
 
 def greet(devices):
@@ -199,24 +186,14 @@
     return (slice(0, first), slice(first, half_width))
 
 
-def gather_kernel(
-    own_ref,
-    wall_ref,
-    twin,
-    wall,
-    twin_sem,
-    step_send,
-    step_recv,
-    pass_send,
-    pass_recv,
-    own_sem,
+def gather_steps(
+    own_ref, twin, wall, twin_sem, step_send, step_recv, pass_send, pass_recv, between
 ):
     at_expert, at_head = lax.axis_index("expert"), lax.axis_index("head")
     low = lax.rem(at_head, 2)
     count = wall.ndim - 3
     bits = my_bits(count, lax.div(at_expert * 4 + at_head, 2))
     sibling = (at_expert, at_head + 1 - 2 * low)
-    greet([sibling] + [across(bits, low, d) for d in range(count)])
     twin_copy = pltpu.make_async_remote_copy(
         src_ref=own_ref,
         dst_ref=twin,
@@ -226,9 +203,7 @@
         device_id_type=MESH,
     )
     twin_copy.start()
-    own_rows = own_ref.shape[0]
     half_width = wall.shape[-1]
-    mine = tuple(bits)
     cols = parts_of(half_width)
     orders = (list(range(count)), list(range(count - 2)) + [count - 1, count - 2])
 
@@ -256,12 +231,13 @@
             device_id_type=MESH,
         )
 
+    between(-1)
     twin_copy.wait()
     first = low == 0
     for side in range(2):
         at = slice(side * half_width, (side + 1) * half_width)
         ours, theirs = own_ref[:, at], twin[:, at]
-        wall[(side,) + mine] = jnp.concatenate(
+        wall[(side,) + tuple(bits)] = jnp.concatenate(
             [jnp.where(first, ours, theirs), jnp.where(first, theirs, ours)], axis=0
         ).astype(BF16)
     for i in range(count):
@@ -272,6 +248,7 @@
         for q in range(2):
             if i:
                 pass_copy(q, i - 1).start()
+        between(i)
     for q in range(2):
         step_copy(q, count - 1).wait_recv()
         pass_copy(q, count - 1).start()
@@ -279,30 +256,116 @@
         for q in range(2):
             step_copy(q, i).wait_send()
             pass_copy(q, i).wait()
-    wall_copy = pltpu.make_async_copy(wall, wall_ref, own_sem)
-    wall_copy.start()
-    wall_copy.wait()
-
-
-def reduce_kernel(
+
+
+def is_me(device):
+    return (device[0] == lax.axis_index("expert")) & (device[1] == lax.axis_index("head"))
+
+
+def hosts(experts):
+    at_expert, at_head = lax.axis_index("expert"), lax.axis_index("head")
+    part, half, low = where_am_i(experts)
+    quarter = experts // 4
+    a, b = lax.div(at_expert, 2 * quarter), lax.rem(lax.div(at_expert, quarter), 2)
+    out = []
+    for k in range(2):
+        r = lax.rem(lax.div(at_head, 2) + k, 2)
+        row = r * 2 * quarter + a * quarter + lax.rem(at_expert, quarter)
+        there = (row, lax.rem(a + b + r, 2) * 2 + low)
+        back = (part, lax.rem(half + k, 2) * 2 + low)
+        out.append((there, back))
+    return out
+
+
+def start_far_first(experts, copies):
+    half = where_am_i(experts)[1]
+    at = lax.rem(lax.div(lax.axis_index("head"), 2) + half, 2)
+    for turn in range(2):
+        for k in range(2):
+
+            @pl.when(lax.rem(at + k + turn, 2) == 1)
+            def _(k=k):
+                for copy in copies[k]:
+                    copy[0]()
+
+
+def maybe_remote(src, dst, send_sem, recv_sem, device, pieces=1):
+    same = is_me(device)
+    rows = src.shape[0] // pieces
+
+    def remote(rows_at=None):
+        return pltpu.make_async_remote_copy(
+            src_ref=src if rows_at is None else src.at[rows_at],
+            dst_ref=dst if rows_at is None else dst.at[rows_at],
+            send_sem=send_sem,
+            recv_sem=recv_sem,
+            device_id=device,
+            device_id_type=MESH,
+        )
+
+    def start():
+        @pl.when(same)
+        def _():
+            pltpu.make_async_copy(src, dst, recv_sem).start()
+
+        @pl.when(jnp.logical_not(same))
+        def _():
+            for i in range(pieces):
+                remote(pl.ds(i * rows, rows)).start()
+
+    def arrived():
+        @pl.when(same)
+        def _():
+            pltpu.make_async_copy(src, dst, recv_sem).wait()
+
+        @pl.when(jnp.logical_not(same))
+        def _():
+            remote().wait_recv()
+
+    def sent():
+        @pl.when(jnp.logical_not(same))
+        def _():
+            remote().wait_send()
+
+    return start, arrived, sent
+
+
+def owners_of(experts):
+    at_expert, at_head = lax.axis_index("expert"), lax.axis_index("head")
+    part, half, low = where_am_i(experts)
+    quarter = experts // 4
+    x = lax.div(at_head, 2)
+    a, b = lax.div(at_expert, 2 * quarter), lax.rem(lax.div(at_expert, quarter), 2)
+    rest = a * quarter + lax.rem(at_expert, quarter)
+    r = lax.rem(x + a + b, 2)
+    return dict(
+        slot=lax.rem(x + half, 2),
+        beside=(at_expert, (1 - x) * 2 + low),
+        direct_to=(part, at_head),
+        passed_to=(flipped(experts, part, quarter), at_head),
+        direct_from=(r * 2 * quarter + rest, at_head),
+        passed_from=((1 - r) * 2 * quarter + rest, at_head),
+    )
+
+
+def reduce_steps(
     all_ref,
     out_ref,
     total,
-    landed,
     last,
     spare,
     pair_sem,
     step_send,
     step_recv,
     last_sem,
-    *landings,
+    landings,
+    between,
 ):
     at_expert, at_head = lax.axis_index("expert"), lax.axis_index("head")
     low = lax.rem(at_head, 2)
     count = all_ref.ndim - 3
     bits = my_bits(count, lax.div(at_expert * 4 + at_head, 2))
     sibling = (at_expert, at_head + 1 - 2 * low)
-    greet([sibling] + [across(bits, low, d) for d in range(count)])
     half_width = all_ref.shape[-1]
     cols = parts_of(half_width)
     backwards = list(range(count))[::-1]
@@ -312,7 +375,7 @@
         at = (slice(None),) * count + (slice(None), cols[q])
         return pltpu.make_async_remote_copy(
             src_ref=all_ref.at[(1 - low,) + at],
-            dst_ref=landed.at[at],
+            dst_ref=total.at[at],
             send_sem=pair_sem.at[q],
             recv_sem=pair_sem.at[2 + q],
             device_id=sibling,
@@ -337,9 +400,10 @@
     for q in range(2):
         at = (slice(None),) * count + (slice(None), cols[q])
         pair_copy(q).wait_recv()
-        total[at] = (all_ref[(low,) + at].astype(F32) + landed[at].astype(F32)).astype(BF16)
+        total[at] = (all_ref[(low,) + at].astype(F32) + total[at].astype(F32)).astype(BF16)
         step_copy(q, 0).start()
     for i in range(count):
+        between(i)
         for q in range(2):
             step_copy(q, i).wait_recv()
             gone, d = orders[q][:i], orders[q][i]
@@ -390,28 +454,61 @@
     )
 
 
+def cut(wall, side, start, stop):
+    rows = wall[(side,) + (slice(None),) * (wall.ndim - 2) + (slice(start, stop),)]
+    return rows.reshape(-1, stop - start)
+
+
 def forward_kernel(
     x_ref,
-    wall_ref,
-    wide_ref,
-    gy_ref,
+    own_ref,
+    wide_in,
+    tall_in,
+    gy_in,
+    inner_ref,
+    outer_ref,
     qkv_ref,
     o_ref,
     h_ref,
     n2_ref,
     p_ref,
     out_ref,
+    wall_ref,
+    w_ref,
+    x_out,
+    gy_out,
+    wide_ref,
+    tall_ref,
     small,
+    stage,
+    masters,
+    both_ref,
     held,
+    twin,
+    wall,
+    twin_sem,
+    step_send,
+    step_recv,
+    pass_send,
+    pass_recv,
     send_sem,
     recv_sem,
+    w_send,
+    w_recv,
+    sib_send,
+    sib_recv,
     own_sem,
+    load_sem,
     *,
     experts,
     cap,
 ):
-    width = x_ref.shape[2]
+    width = x_ref.shape[1]
     part, half, low = where_am_i(experts)
+    at_expert, at_head = lax.axis_index("expert"), lax.axis_index("head")
+    sibling = (at_expert, at_head + 1 - 2 * low)
+    count = wall.ndim - 3
+    bits = my_bits(count, lax.div(at_expert * 4 + at_head, 2))
 
     def swap_copy(k):
         return pltpu.make_async_remote_copy(
@@ -423,26 +520,88 @@
             device_id_type=MESH,
         )
 
-    own_copy = pltpu.make_async_copy(held.at[0], out_ref.at[0], own_sem)
+    pieces = w_send.shape[0] // 2
+    piece = 2 * width // pieces
+
+    def sib_copy(k, j):
+        at = pl.ds(j * piece, piece)
+        return pltpu.make_async_remote_copy(
+            src_ref=w_ref.at[k, at],
+            dst_ref=w_ref.at[2 + k, at],
+            send_sem=sib_send.at[k * pieces + j],
+            recv_sem=sib_recv.at[k * pieces + j],
+            device_id=sibling,
+            device_id_type=MESH,
+        )
+
+    w_copies = [
+        [
+            maybe_remote(
+                both_ref.at[pl.ds(j * piece, piece)],
+                w_ref.at[k, pl.ds(j * piece, piece)],
+                w_send.at[k * pieces + j],
+                w_recv.at[k * pieces + j],
+                there,
+                2,
+            )
+            for j in range(pieces)
+        ]
+        for k, (there, _) in enumerate(hosts(experts))
+    ]
+    early = early_parts(experts)
+    own_copy = pltpu.make_async_copy(held.at[0], out_ref.at[0], own_sem.at[0])
+    wall_copy = pltpu.make_async_copy(wall, wall_ref, own_sem.at[1])
 
     @pl.when(pl.program_id(0) == 0)
     def _():
-        greet([partner(experts, part, half, low, k) for k in range(1, experts)])
-        rows = gy_ref[...]
-        for k in range(experts - 1, 0, -1):
-            held[k] = picked_rows(wide_ref, rows, k, cap)
-            swap_copy(k).start()
-        held[0] = picked_rows(wide_ref, rows, 0, cap)
-        own_copy.start()
-        small[...] = wall_ref[0, :, 2 * width :].astype(F32).T
-
-    x = x_ref[0].astype(F32)
+        loads = [
+            pltpu.make_async_copy(ref, masters.at[pl.ds(j * width, width), :], load_sem.at[j])
+            for j, ref in enumerate((inner_ref, outer_ref))
+        ]
+        for load in loads:
+            load.start()
+        greet(
+            [sibling]
+            + [across(bits, low, d) for d in range(count)]
+            + [partner(experts, part, half, low, k) for k in range(1, experts)]
+            + [device for pair in hosts(experts) for device in pair]
+        )
+
+        def send_blocks(blocks):
+            rows = gy_out[...].reshape(-1, width)
+            for k in blocks:
+                held[k] = picked_rows(wide_ref, rows, k, cap)
+                (swap_copy(k) if k else own_copy).start()
+
+        def between(i):
+            if i < 0:
+                route(part, wide_in, tall_in, wide_ref, tall_ref, experts, cap)
+            if i == 0:
+                for load in loads:
+                    load.wait()
+                both_ref[...] = masters[...].astype(BF16)
+                spread_images(stage, gy_in[...], gy_out)
+            if 0 <= i < len(early):
+                send_blocks(early[i])
+            if i == 1:
+                start_far_first(experts, w_copies)
+            if i == 2:
+                spread_images(stage, x_ref[...], x_out)
+
+        gather_steps(
+            own_ref, twin, wall, twin_sem, step_send, step_recv, pass_send, pass_recv, between
+        )
+        wall_copy.start()
+        send_blocks([0])
+        small[...] = cut(wall, 0, 2 * width, 2 * width + 128).astype(F32).T
+
+    x = x_out[pl.program_id(0)].astype(F32)
     gain, shift = small[experts : experts + 1, :], small[experts + 1 : experts + 2, :]
     unit, _ = norm_parts(x)
     n1 = (unit * gain + shift).astype(BF16)
     for j in range(3):
         qkv_ref[0, :, j * width : (j + 1) * width] = dot_nn(
-            n1, wall_ref[j // 2, :, (j % 2) * width : (j % 2 + 1) * width]
+            n1, cut(wall, j // 2, (j % 2) * width, (j % 2 + 1) * width)
         ).astype(BF16)
     lane = lax.broadcasted_iota(jnp.int32, (PAD, 128), 1)
     key_at = lax.broadcasted_iota(jnp.int32, (PAD, PAD), 1)
@@ -461,7 +620,7 @@
         o_ref[0, :, pair * 128 : (pair + 1) * 128] = jnp.where(
             lane < HD, halves[0], halves[1]
         ).astype(BF16)
-    h = x + dot_nn(o_ref[0], wall_ref[1, :, width : 2 * width])
+    h = x + dot_nn(o_ref[0], cut(wall, 1, width, 2 * width))
     h_ref[0] = h
     gain, shift = small[experts + 2 : experts + 3, :], small[experts + 3 : experts + 4, :]
     unit, _ = norm_parts(h)
@@ -473,26 +632,29 @@
 
     @pl.when(pl.program_id(0) == pl.num_programs(0) - 1)
     def _():
-        for k in range(1, experts):
+        for j in range(pieces):
+            for k in range(2):
+                w_copies[k][j][1]()
+                sib_copy(k, j).start()
+        for k in sum(early, []):
             swap_copy(k).wait()
         own_copy.wait()
+        wall_copy.wait()
+        for j in range(pieces):
+            for k in range(2):
+                w_copies[k][j][2]()
+                sib_copy(k, j).wait()
 
 
 def expert_kernel(
     wide_ref,
     rows_ref,
     g_ref,
-    w0_ref,
-    w1_ref,
-    w2_ref,
-    w3_ref,
+    w_ref,
     router_ref,
     y_ref,
     dr_ref,
-    in0_ref,
-    out0_ref,
-    in1_ref,
-    out1_ref,
+    pair_ref,
     x_all,
     g_all,
     held,
@@ -519,7 +681,6 @@
     at_expert, at_head = lax.axis_index("expert"), lax.axis_index("head")
     sibling = (at_expert, at_head + 1 - 2 * low)
     greet([partner(experts, part, half, low, k) for k in range(1, experts)] + [sibling])
-    sequence = [block_at(experts, j) for j in range(experts)]
     width = x_all.shape[2]
     slice_width = w_all.shape[2]
     tile = group * cap
@@ -548,15 +709,15 @@
         )
 
     weights = [
-        pltpu.make_async_copy(w, w_all.at[j], w_sem.at[j])
-        for j, w in enumerate((w0_ref, w1_ref, w2_ref, w3_ref))
+        pltpu.make_async_copy(w_ref.at[j], w_all.at[j], w_sem.at[j]) for j in range(4)
     ]
     for copy in weights:
         copy.start()
     g_copy = pltpu.make_async_copy(g_ref, g_all, g_sem)
     g_copy.start()
     rows = rows_ref[...]
-    for k in sequence:
+    turns = sequence(experts)
+    for k in turns:
         if k:
             held[k] = picked_rows(wide_ref, rows, k, cap)
             x_copy(k).start()
@@ -674,12 +835,8 @@
         for side in range(2):
             at = slice(side * width, (side + 1) * width)
             w_all[2 + j, at, :] = (w_all[2 + j, at, :].astype(F32) + acc[j, side]).astype(BF16)
-        for side, ref in enumerate(((in0_ref, out0_ref), (in1_ref, out1_ref))[j]):
-            at = pl.ds(side * width, width)
-            results.append(
-                pltpu.make_async_copy(w_all.at[2 + j, at, :], ref, w_sem.at[2 * j + side])
-            )
-            results[-1].start()
+        results.append(pltpu.make_async_copy(w_all.at[2 + j], pair_ref.at[j], w_sem.at[j]))
+        results[-1].start()
     for copy in results:
         copy.wait()
 
@@ -705,9 +862,12 @@
     wall_ref,
     dr_ref,
     y_ref,
+    pair_ref,
     grad_ref,
-    all_ref,
     out_ref,
+    shared_ref,
+    back_ref,
+    beside_ref,
     small,
     acc,
     small_acc,
@@ -717,7 +877,17 @@
     send_sem,
     recv_sem,
     own_sem,
-    *,
+    g_send,
+    g_recv,
+    all_ref,
+    total,
+    last,
+    spare,
+    pair_sem,
+    step_send,
+    step_recv,
+    last_sem,
+    *landings,
     experts,
     cap,
 ):
@@ -736,12 +906,56 @@
         )
 
     own_copy = pltpu.make_async_copy(y_ref.at[0], y_in.at[0], own_sem)
+    at_expert, at_head = lax.axis_index("expert"), lax.axis_index("head")
+    sibling = (at_expert, at_head + 1 - 2 * low)
+    count = all_ref.ndim - 3
+    bits = my_bits(count, lax.div(at_expert * 4 + at_head, 2))
+    ways = owners_of(experts)
+    slot_at = ways["slot"]
+    direct = maybe_remote(
+        pair_ref.at[slot_at],
+        back_ref.at[slot_at],
+        g_send.at[0],
+        g_recv.at[0],
+        ways["direct_to"],
+        12,
+    )
+    turns = beside_ref.shape[0]
+    piece = beside_ref.shape[1]
+    aside = [
+        pltpu.make_async_remote_copy(
+            src_ref=pair_ref.at[1 - slot_at, pl.ds(j * piece, piece)],
+            dst_ref=beside_ref.at[j],
+            send_sem=g_send.at[1 + j],
+            recv_sem=g_recv.at[1 + j],
+            device_id=ways["beside"],
+            device_id_type=MESH,
+        )
+        for j in range(turns)
+    ]
+    passed = [
+        maybe_remote(
+            beside_ref.at[j],
+            back_ref.at[slot_at, pl.ds(j * piece, piece)],
+            g_send.at[1 + turns + j],
+            g_recv.at[1 + turns + j],
+            ways["passed_to"],
+            3,
+        )
+        for j in range(turns)
+    ]
 
     @pl.when(step == 0)
     def _():
-        greet([partner(experts, part, half, low, k) for k in range(1, experts)])
-        for k in range(experts - 1, 0, -1):
-            swap_copy(k).start()
+        greet(
+            [sibling, ways["beside"]]
+            + [across(bits, low, d) for d in range(count)]
+            + [partner(experts, part, half, low, k) for k in range(1, experts)]
+            + [ways["direct_to"], ways["passed_to"], ways["direct_from"], ways["passed_from"]]
+        )
+        for j in range(turns):
+            aside[j].start()
+        direct[0]()
         own_copy.start()
         small[...] = wall_ref[0, :, 2 * width :].astype(F32).T
         acc[...] = jnp.zeros_like(acc)
@@ -776,7 +990,7 @@
     small_acc[experts + 3 : experts + 4, :] += jnp.sum(dn2, axis=0, keepdims=True)
     dh = gy + norm_back(dn2, unit, spread, gain)
     dh_low = dh.astype(BF16)
-    acc[:, 3 * width :] += dot_tn(o_ref[0], dh_low)
+    acc[0:width, 3 * width :] += dot_tn(o_ref[0], dh_low)
     do = dot_nt(dh_low, wall_ref[1, :, width : 2 * width]).astype(BF16)
 
     lane = lax.broadcasted_iota(jnp.int32, (PAD, 128), 1)
@@ -810,61 +1024,101 @@
     dn1 = jnp.zeros((PAD, width), F32)
     for j in range(3):
         cols = slice(j * width, (j + 1) * width)
-        acc[:, cols] += dot_tn(n1, dqkv[:, cols])
+        acc[0:width, cols] += dot_tn(n1, dqkv[:, cols])
         dn1 = dn1 + dot_nt(
             dqkv[:, cols], wall_ref[j // 2, :, (j % 2) * width : (j % 2 + 1) * width]
         )
     small_acc[experts : experts + 1, :] += jnp.sum(dn1 * unit, axis=0, keepdims=True)
     small_acc[experts + 1 : experts + 2, :] += jnp.sum(dn1, axis=0, keepdims=True)
-    grad_ref[0] = dh + norm_back(dn1, unit, spread, gain)
+    grad = dh + norm_back(dn1, unit, spread, gain)
+    images = tall_ref.shape[0]
+    for i in range(images):
+
+        @pl.when(step == i)
+        def _(i=i):
+            grad_ref[i * SEQ : (i + 1) * SEQ, :] = grad[0:SEQ, :]
+
+    for j in range(turns):
+
+        @pl.when(step == j)
+        def _(j=j):
+            aside[j].wait_recv()
+            passed[j][0]()
+            for k in list(range(experts - 1, 0, -1))[j::turns]:
+                swap_copy(k).start()
 
     @pl.when(step == pl.num_programs(0) - 1)
     def _():
+        blocks = all_ref.shape[1:-1]
+        everything = (slice(None),) * len(blocks)
         for j in range(4):
-            all_ref[j // 2, :, (j % 2) * width : (j % 2 + 1) * width] = acc[
-                :, j * width : (j + 1) * width
-            ].astype(BF16)
-        all_ref[0, :, 2 * width :] = small_acc[...].T.astype(BF16)
-        all_ref[1, :, 2 * width :] = jnp.zeros((width, 128), BF16)
-        for k in range(1, experts):
-            swap_copy(k).wait()
-        own_copy.wait()
-
-        def one_image(image, _):
-            total = h_ref[image]
+            all_ref[(j // 2,) + everything + (slice((j % 2) * width, (j % 2 + 1) * width),)] = (
+                acc[0:width, j * width : (j + 1) * width].astype(BF16).reshape(blocks + (width,))
+            )
+        rest = (slice(2 * width, 2 * width + 128),)
+        all_ref[(0,) + everything + rest] = (
+            small_acc[...].T.astype(BF16).reshape(blocks + (128,))
+        )
+        all_ref[(1,) + everything + rest] = jnp.zeros(blocks + (128,), BF16)
+
+        def one_image(image):
+            mixed = h_ref[image]
             for k in range(experts):
-                total = total + dot_nn(owners(image, k), y_in[k])
-            out_ref[image] = total.astype(BF16)
-            return 0
-
-        lax.fori_loop(0, out_ref.shape[0], one_image, 0)
-
-
-def adam_kernel(m_ref, f_ref, q_ref, a_ref, b_ref, w_out, f_out, q_out, c_out, *, rate, turn):
-    grad = a_ref[...].astype(F32) + b_ref[...].astype(F32)
-    if turn:
-        grad = grad.T
-    new = adam_step(m_ref[...], f_ref[...], q_ref[...], grad, rate)
-    w_out[...], f_out[...], q_out[...], c_out[...] = new
-
-
-def expert_adam(master, first_state, square, grads, rate, turn):
-    shape = master.shape
-    rows, cols = shape[1], shape[2]
-    block = 128
-    here = pl.BlockSpec((block, cols), lambda i: (i, 0))
-    there = pl.BlockSpec((cols, block), lambda i: (0, i)) if turn else here
-    new = pl.pallas_call(
-        functools.partial(adam_kernel, rate=rate, turn=turn),
-        grid=(rows // block,),
-        out_shape=[jax.ShapeDtypeStruct((rows, cols), t) for t in (F32, F32, F32, BF16)],
-        in_specs=[here, here, here, there, there],
-        out_specs=[here] * 4,
-        compiler_params=params(),
-        cost_estimate=cost(9),
-        name="adam",
-    )(*(v.reshape(rows, cols) for v in (master, first_state, square)), *grads)
-    return tuple(v.reshape(shape) for v in new)
+                mixed = mixed + dot_nn(owners(image, k), y_in[k])
+            acc[image * SEQ : (image + 1) * SEQ, 0:width] = mixed[0:SEQ, :]
+
+        def between(i):
+            if i == count - 1:
+                for k in range(1, experts):
+                    swap_copy(k).wait()
+                own_copy.wait()
+                for image in range(images):
+                    one_image(image)
+                out_ref[...] = acc[0 : out_ref.shape[0], 0:width].astype(BF16)
+
+        reduce_steps(
+            all_ref,
+            shared_ref,
+            total,
+            last,
+            spare,
+            pair_sem,
+            step_send,
+            step_recv,
+            last_sem,
+            landings,
+            between,
+        )
+        for j in range(turns):
+            aside[j].wait_send()
+            passed[j][1]()
+            passed[j][2]()
+        direct[1]()
+        direct[2]()
+
+
+def adam_kernel(*refs, rates, shapes):
+    ins, outs = refs[: len(refs) - 24], refs[len(refs) - 24 :]
+    inner, outer = ins[0:3], ins[3:6]
+    a0, a1, b0, b1 = ins[6:10]
+    shared = ins[10:22]
+    qkv_grad, router_grad, norm_grad, shared_grad = ins[22:26]
+
+    def put(at, masters, grad, rate):
+        new = adam_step(*(m[...] for m in masters), grad, rate)
+        for j in range(4):
+            outs[at + j][...] = new[j]
+
+    put(16, inner, a0[0].astype(F32) + a1[0].astype(F32), rates[4])
+    put(20, outer, (b0[0].astype(F32) + b1[0].astype(F32)).T, rates[5])
+
+    @pl.when(pl.program_id(0) == 0)
+    def _():
+        proj = shapes
+        put(0, shared[0:3], qkv_grad[...], rates[0])
+        put(4, shared[3:6], shared_grad[:, proj[0] : proj[1]], rates[1])
+        put(8, shared[6:9], router_grad[...], rates[2])
+        put(12, shared[9:12], norm_grad[...], rates[3])
 
 
 def on_device(
@@ -908,8 +1162,6 @@
     anywhere = pl.BlockSpec(memory_space=pl.ANY)
     struct = jax.ShapeDtypeStruct
 
-    ids = where_am_i(experts)[0].reshape(1).astype(jnp.int32)
-
     qkv_own = qkv_master.reshape(own_rows, heads, 3, HD).transpose(0, 2, 1, 3)
     qkv_own = qkv_own.reshape(own_rows, 3 * width)
     wall_own = jnp.concatenate(
@@ -927,48 +1179,11 @@
     half_width = 2 * width + 128
     count = (width // own_rows).bit_length() - 2
     block = (2,) * count + (2 * own_rows, half_width)
-    in_kernel = own_rows % 8 == 0
-
-    both = jnp.concatenate([inner_master[0].astype(BF16), outer_master[0].astype(BF16)], axis=0)
-    w_own = [lax.ppermute(both, AXES, weight_perm(experts, k)) for k in range(2)]
-
-    def padded(values):
-        return jnp.pad(values.reshape(images, SEQ, -1), ((0, 0), (0, PAD - SEQ), (0, 0)))
 
     tall = jnp.pad(
         routes.reshape(images, SEQ, 2), ((0, 0), (0, PAD - SEQ), (0, 0)), constant_values=-1
     ).reshape(tokens, 2)
-    wide_slots, tall_slots = pl.pallas_call(
-        functools.partial(routing_kernel, experts=experts, cap=cap),
-        out_shape=(struct((2, tokens), jnp.int32), struct((tokens, 2), jnp.int32)),
-        in_specs=[smem, vmem, vmem],
-        out_specs=(vmem, vmem),
-        compiler_params=params(),
-        name="routing",
-    )(ids, tall.T, tall)
-    tall_slots = tall_slots.reshape(images, PAD, 2)
-
-    gy = padded(output_grad)
     dma = pltpu.SemaphoreType.DMA
-    wall = pl.pallas_call(
-        gather_kernel,
-        out_shape=struct((2,) + block, BF16),
-        in_specs=[vmem],
-        out_specs=anywhere,
-        scratch_shapes=[
-            pltpu.VMEM(wall_own.shape, F32),
-            pltpu.VMEM((2,) + block, BF16),
-            dma((2,)),
-        ]
-        + [dma((2, count))] * 4
-        + [dma],
-        compiler_params=params(collective_id=0, has_side_effects=True),
-        cost_estimate=cost(50),
-        name="gather_shared",
-    )(wall_own)
-    wall = wall.reshape(2, width, half_width)
-
-    x = padded(block_input)
 
     def image_spec(*dims):
         return pl.BlockSpec((1,) + dims, lambda i: (i,) + (0,) * len(dims))
@@ -977,55 +1192,86 @@
         mode = dict(pipeline_mode=pl.Buffered(1)) if once else {}
         return pl.BlockSpec(dims, lambda i: (0,) * len(dims), **mode)
 
-    qkv, attended, middle, second, probs, g_blocks = pl.pallas_call(
-        functools.partial(forward_kernel, experts=experts, cap=cap),
-        grid=(images,),
-        out_shape=(
-            struct((images, PAD, 3 * width), BF16),
-            struct((images, PAD, width), BF16),
-            struct((images, PAD, width), F32),
-            struct((images, PAD, width), BF16),
-            struct((images, experts, PAD), F32),
-            struct((experts, cap, width), BF16),
-        ),
-        in_specs=[
-            image_spec(PAD, width),
-            whole_spec(2, width, half_width),
-            whole_spec(2, tokens),
-            whole_spec(tokens, width),
-        ],
-        out_specs=(
-            image_spec(PAD, 3 * width),
-            image_spec(PAD, width),
-            image_spec(PAD, width),
-            image_spec(PAD, width),
-            image_spec(experts, PAD),
-            anywhere,
-        ),
-        scratch_shapes=[
-            pltpu.VMEM((128, width), F32),
-            pltpu.VMEM((experts, cap, width), BF16),
-            dma((experts,)),
-            dma((experts,)),
-            dma,
-        ],
-        compiler_params=params(collective_id=3, has_side_effects=True),
-        cost_estimate=cost(50),
-        name="forward",
-    )(x, wall, wide_slots, gy.reshape(tokens, width))
-
-    w_own_late, second = lax.optimization_barrier((w_own, second))
-    w_sib = [lax.ppermute(w, AXES, core_perm(experts)) for w in w_own_late]
+    qkv, attended, middle, second, probs, g_blocks, wall, w_all, x, gy, wide_slots, tall_slots = (
+        pl.pallas_call(
+            functools.partial(forward_kernel, experts=experts, cap=cap),
+            grid=(images,),
+            out_shape=(
+                struct((images, PAD, 3 * width), BF16),
+                struct((images, PAD, width), BF16),
+                struct((images, PAD, width), F32),
+                struct((images, PAD, width), BF16),
+                struct((images, experts, PAD), F32),
+                struct((experts, cap, width), BF16),
+                struct((2,) + block, BF16),
+                struct((4, 2 * width, slice_width), BF16),
+                struct((images, PAD, width), BF16),
+                struct((images, PAD, width), BF16),
+                struct((2, tokens), jnp.int32),
+                struct((images, PAD, 2), jnp.int32),
+            ),
+            in_specs=[
+                whole_spec(row_count, width),
+                whole_spec(*wall_own.shape),
+                whole_spec(2, tokens),
+                whole_spec(tokens, 2),
+                whole_spec(row_count, width),
+                anywhere,
+                anywhere,
+            ],
+            out_specs=(
+                image_spec(PAD, 3 * width),
+                image_spec(PAD, width),
+                image_spec(PAD, width),
+                image_spec(PAD, width),
+                image_spec(experts, PAD),
+                anywhere,
+                anywhere,
+                anywhere,
+                whole_spec(images, PAD, width, once=False),
+                whole_spec(images, PAD, width, once=False),
+                whole_spec(2, tokens, once=False),
+                whole_spec(images, PAD, 2, once=False),
+            ),
+            scratch_shapes=[
+                pltpu.VMEM((128, width), F32),
+                pltpu.VMEM((tokens, width), F32),
+                pltpu.VMEM((2 * width, slice_width), F32),
+                pltpu.VMEM((2 * width, slice_width), BF16),
+                pltpu.VMEM((experts, cap, width), BF16),
+                pltpu.VMEM(wall_own.shape, F32),
+                pltpu.VMEM((2,) + block, BF16),
+                dma((2,)),
+            ]
+            + [dma((2, count))] * 4
+            + [dma((experts,))] * 2
+            + [dma((8,))] * 4
+            + [dma((2,))] * 2,
+            compiler_params=params(collective_id=0, has_side_effects=True),
+            cost_estimate=cost(120),
+            name="forward",
+        )(
+            block_input,
+            wall_own,
+            tall.T,
+            tall,
+            output_grad,
+            inner_master.reshape(width, slice_width),
+            outer_master.reshape(slice_width, width),
+        )
+    )
+    wall = wall.reshape(2, width, half_width)
+
     router_low = wall[0, :, 2 * width : 2 * width + experts].T
-    y_blocks, dr_blocks, in0, out0, in1, out1 = pl.pallas_call(
+    y_blocks, dr_blocks, grad_pair = pl.pallas_call(
         functools.partial(expert_kernel, experts=experts, cap=cap, group=group),
         out_shape=(
             struct((experts, cap, width), BF16),
             struct((experts, cap + 16, width), BF16),
-        )
-        + (struct((width, slice_width), BF16),) * 4,
-        in_specs=[vmem, vmem] + [anywhere] * 5 + [vmem],
-        out_specs=[anywhere] * 6,
+            struct((2, 2 * width, slice_width), BF16),
+        ),
+        in_specs=[vmem, vmem, anywhere, anywhere, vmem],
+        out_specs=[anywhere] * 3,
         scratch_shapes=[
             pltpu.VMEM((experts, cap + 16, width), BF16),
             pltpu.VMEM((experts, cap, width), BF16),
@@ -1040,20 +1286,28 @@
         compiler_params=params(collective_id=1, has_side_effects=True),
         cost_estimate=cost(140),
         name="experts",
-    )(wide_slots, second.reshape(tokens, width), g_blocks, *w_own_late, *w_sib, router_low)
-
-    grad_back = [
-        [lax.ppermute(g, AXES, turned(weight_perm(experts, k))) for k, g in enumerate(pair)]
-        for pair in ((in0, in1), (out0, out1))
+    )(
+        wide_slots,
+        second.reshape(tokens, width),
+        g_blocks,
+        w_all,
+        router_low,
+    )
+
+    landings = [
+        pltpu.VMEM((2,) * (count - 1 - i) + (2 * own_rows, c.stop - c.start), BF16)
+        for c in parts_of(half_width)
+        for i in range(count)
     ]
-
-    input_grad, shared_grad, block_output = pl.pallas_call(
+    input_grad, block_output, shared_own, grad_back, _ = pl.pallas_call(
         functools.partial(backward_kernel, experts=experts, cap=cap),
         grid=(images,),
         out_shape=(
-            struct((images, PAD, width), F32),
-            struct((2, width, half_width), BF16),
-            struct((images, PAD, width), BF16),
+            struct((row_count, width), F32),
+            struct((row_count, width), BF16),
+            struct((own_rows, 2 * half_width), F32),
+            struct((2, 2 * width, slice_width), BF16),
+            struct((images, 2 * width // images, slice_width), BF16),
         ),
         in_specs=[
             whole_spec(images, PAD, 2),
@@ -1066,15 +1320,18 @@
             whole_spec(2, width, half_width),
             whole_spec(experts, cap + 16, width),
             anywhere,
+            anywhere,
         ],
         out_specs=(
-            image_spec(PAD, width),
-            whole_spec(2, width, half_width, once=False),
-            whole_spec(images, PAD, width, once=False),
+            whole_spec(row_count, width),
+            whole_spec(row_count, width),
+            whole_spec(own_rows, 2 * half_width),
+            anywhere,
+            anywhere,
         ),
         scratch_shapes=[
             pltpu.VMEM((128, width), F32),
-            pltpu.VMEM((width, 4 * width), F32),
+            pltpu.VMEM((max(width, row_count + 7 & -8), 4 * width), F32),
             pltpu.VMEM((128, width), F32),
             pltpu.VMEM((PAD, 3 * width), BF16),
             pltpu.VMEM((experts, PAD), F32),
@@ -1082,26 +1339,9 @@
             dma((experts,)),
             dma((experts,)),
             dma,
-        ],
-        compiler_params=params(collective_id=4, has_side_effects=True),
-        cost_estimate=cost(60),
-        name="backward",
-    )(tall_slots, gy, x, middle, qkv, attended, probs, wall, dr_blocks, y_blocks)
-    input_grad = input_grad[:, :SEQ].reshape(row_count, width)
-    block_output = block_output[:, :SEQ].reshape(row_count, width)
-
-    landings = [
-        pltpu.VMEM((2,) * (count - 1 - i) + (2 * own_rows, c.stop - c.start), BF16)
-        for c in parts_of(half_width)
-        for i in range(count)
-    ]
-    shared_own = pl.pallas_call(
-        reduce_kernel,
-        out_shape=struct((own_rows, 2 * half_width), F32),
-        in_specs=[vmem],
-        out_specs=vmem,
-        scratch_shapes=[
-            pltpu.VMEM(block, BF16),
+            dma((1 + 2 * images,)),
+            dma((1 + 2 * images,)),
+            pltpu.VMEM((2,) + block, BF16),
             pltpu.VMEM(block, BF16),
             pltpu.VMEM((2 * own_rows, half_width), F32),
             pltpu.VMEM((2, own_rows, half_width), F32),
@@ -1112,46 +1352,83 @@
         ]
         + landings,
         compiler_params=params(collective_id=2, has_side_effects=True),
-        cost_estimate=cost(50),
-        name="reduce_shared",
-    )(shared_grad.reshape((2,) + block))
+        cost_estimate=cost(120),
+        name="backward",
+    )(tall_slots, gy, x, middle, qkv, attended, probs, wall, dr_blocks, y_blocks, grad_pair)
+
     qkv_owned = jnp.concatenate(
         [shared_own[:, : 2 * width], shared_own[:, half_width : half_width + width]], axis=1
     )
     qkv_owned = qkv_owned.reshape(own_rows, 3, heads, HD).transpose(0, 2, 1, 3)
     qkv_owned = qkv_owned.reshape(own_rows, 3 * width)
-    proj_owned = shared_own[:, half_width + width : half_width + 2 * width]
-    router_owned = shared_own[:, 2 * width : 2 * width + experts]
-    norm_owned = shared_own[:, 2 * width + experts : 2 * width + experts + 4].T
-
-    qkv_new = adam_step(qkv_master, qkv_mean, qkv_square, qkv_owned, 2.0 * width ** (-0.5))
-    proj_new = adam_step(
-        proj_master, proj_mean, proj_square, proj_owned, 2.0 * (width // 16) ** (-0.5)
+    small_owned = shared_own[:, 2 * width : 2 * width + experts + 4].T
+    small_owned = [small_owned[:experts], small_owned[experts:]]
+
+    rates = (
+        2.0 * width ** (-0.5),
+        2.0 * (width // 16) ** (-0.5),
+        2.0 * (4 * width) ** (-0.5),
+        NORM_RATE,
+        2.0 * width ** (-0.5),
+        2.0 * max(1, FF * 4 // (experts * experts)) ** (-0.5),
     )
-    router_new = adam_step(
-        router_master, router_mean, router_square, router_owned, 2.0 * (4 * width) ** (-0.5)
-    )
-    norm_new = adam_step(norm_master, norm_mean, norm_square, norm_owned, NORM_RATE)
-    inner_new = expert_adam(
-        inner_master, inner_mean, inner_square, grad_back[0], 2.0 * width ** (-0.5), False
-    )
-    outer_new = expert_adam(
-        outer_master,
-        outer_mean,
-        outer_square,
-        grad_back[1],
-        2.0 * max(1, FF * 4 // (experts * experts)) ** (-0.5),
-        True,
-    )
+    step_rows = 128
+
+    def rows_spec(cols):
+        return pl.BlockSpec((step_rows, cols), lambda i: (i, 0))
+
+    shared = [
+        qkv_master,
+        qkv_mean,
+        qkv_square,
+        proj_master,
+        proj_mean,
+        proj_square,
+        router_master.T,
+        router_mean.T,
+        router_square.T,
+        norm_master,
+        norm_mean,
+        norm_square,
+    ]
+    inner = [v.reshape(width, slice_width) for v in (inner_master, inner_mean, inner_square)]
+    outer = [v.reshape(slice_width, width) for v in (outer_master, outer_mean, outer_square)]
+    state = []
+    for v in shared[::3] + [inner[0], outer[0]]:
+        state += [struct(v.shape, t) for t in (F32, F32, F32, BF16)]
+    new = pl.pallas_call(
+        functools.partial(
+            adam_kernel,
+            rates=rates,
+            shapes=(half_width + width, half_width + 2 * width),
+        ),
+        grid=(width // step_rows,),
+        out_shape=state,
+        in_specs=[rows_spec(slice_width)] * 3
+        + [rows_spec(width)] * 3
+        + [
+            pl.BlockSpec((1, step_rows, slice_width), functools.partial(lambda k, i: (k, i, 0), k))
+            for k in range(2)
+        ]
+        + [
+            pl.BlockSpec((1, width, step_rows), functools.partial(lambda k, i: (k, 1, i), k))
+            for k in range(2)
+        ]
+        + [whole_spec(*v.shape) for v in shared + [qkv_owned] + small_owned + [shared_own]],
+        out_specs=[whole_spec(*v.shape, once=False) for v in state[:16]]
+        + [rows_spec(slice_width)] * 4
+        + [rows_spec(width)] * 4,
+        compiler_params=params(),
+        cost_estimate=cost(15),
+        name="adam",
+    )(*inner, *outer, *([grad_back] * 4), *shared, qkv_owned, *small_owned, shared_own)
     return (
         block_output,
         input_grad,
-        *qkv_new,
-        *proj_new,
-        *router_new,
-        *norm_new,
-        *inner_new,
-        *outer_new,
+        *new[:8],
+        *(v.T for v in new[8:12]),
+        *new[12:16],
+        *(v[None] for v in new[16:]),
     )
 
 

time: 612 us -> 477 us (0.78)
  the two profiles are of different devices: /device:TPU:0 before, /device:TPU:7 now
where the time goes in v2:
time: 477 us; the launch traced here: 469 us
  Pallas kernels  452 us (95%)
  local copies, waits for them, and re-layouts  15.7 us (3%)
    pallas_call x1, Pallas kernels, on_device(): pl.pallas_call(functools.partial(backward_kernel, experts=experts, cap=ca...  155 us
    pallas_call x1, Pallas kernels, on_device(): pl.pallas_call(functools.partial(forward_kernel, experts=experts, cap=cap...  155 us
    pallas_call x1, Pallas kernels, on_device(): pl.pallas_call(functools.partial(expert_kernel, experts=experts, cap=cap,...  125 us
    pallas_call x1, Pallas kernels, on_device(): pl.pallas_call(functools.partial(adam_kernel, rates=rates, shapes=(half_w...  16.7 us

profile of v2, /device:TPU:7, one launch (start us, length us, event | category | flops | bytes accessed | tf_op | source)
XLA Modules:
  0.0 468.6 jit_solution(16663399463138959220)
XLA Ops:
  0.7 0.8 reshape.98
  1.4 0.8 copy.57
  2.2 0.8 copy.56
  3.0 0.2 copy.58
  3.2 0.0 copy-start.4
  3.2 0.0 copy-start.1
  3.2 0.8 copy.59.wide_in
  4.0 1.2 reshape.96
  5.3 0.1 copy.55
  5.3 0.1 reshape.97
  5.5 0.0 copy-done.4
  5.5 0.8 concatenate.6.own_ref
  6.3 0.0 copy-done.1
  6.3 154.7 %forward.1 = (bf16[4,208,2304]{2,1,0:T(8,128)(2,1)}, bf16[4,208,768]{2,1,0:T(8,128)(2,1)}, f32[4,208,768]{2,1,0:T(8,128)}, bf16[4,208,768]{2,1,0:T(8,128)(2,1)},...) custom-call(bf16[788,768]{1,0:T(8,128)(2,1)} %x_ref.1, ...), custom_call_target="tpu_custom_call" | custom-call | flops 131999997952 | bytes 360000000 | tf_op jit(solution)/shard_map/forward/pallas_call | solution.py:1196
  161.1 0.9 slice_bitcast_fusion
  162.0 0.7 copy.60.router_ref
  162.7 125.4 %experts.1 = (bf16[8,320,768]{2,1,0:T(8,128)(2,1)}, bf16[8,336,768]{2,1,0:T(8,128)(2,1)}, bf16[2,1536,768]{2,1,0:T(8,128)(2,1)}) custom-call(s32[2,832]{1,0:T(2,128)} %get-tuple-element.77.wide_ref, bf16[832,768]{1,0:T(8,128)(2,1)} %bitcast.61, bf16[8,320,768]{2,1,0:T(8,128)(2,1)} %get-tuple-element.79.g_ref, bf16[4,1536,768]{2,1,0:T(8,128)(2,1)} %get-tuple-element.80.w_ref, ...), custom_call_target="tpu_custom_call" | custom-call | flops 153999998976 | bytes 420000000 | tf_op jit(solution)/shard_map/experts/pallas_call | solution.py:1266
  288.1 155.0 %backward.1 = (f32[788,768]{1,0:T(8,128)}, bf16[788,768]{1,0:T(8,128)(2,1)}, f32[24,3328]{1,0:T(8,128)}, bf16[2,1536,768]{2,1,0:T(8,128)(2,1)}, bf16[4,384,768]{2,1,0:T(8,128)(2,1)}) custom-call(s32[4,208,2]{2,1,0:T(8,128)} %get-tuple-element.69.tall_ref, bf16[4,208,768]{2,1,0:T(8,128)(2,1)} %get-tuple-element.70.gy_ref, ...), custom_call_target="tpu_custom_call" | custom-call | flops 131999997952 | bytes 360000000 | tf_op jit(solution)/shard_map/backward/pallas_call | solution.py:1302
  443.2 0.0 copy-start.3
  443.2 1.0 slice.28
  444.1 0.9 slice.27
  445.1 0.1 reshape.108
  445.2 0.2 copy.61
  445.4 1.1 reshape.109.refs_22_
  446.5 0.0 copy-done.3
  446.5 0.5 copy.62
  447.0 0.5 slice.37.refs_24_
  447.6 0.6 slice.36.refs_23_
  448.2 0.0 copy-start.2
  448.2 16.7 %adam.1 = (f32[24,2304]{1,0:T(8,128)}, f32[24,2304]{1,0:T(8,128)}, f32[24,2304]{1,0:T(8,128)}, bf16[24,2304]{1,0:T(8,128)(2,1)}, f32[24,768]{1,0:T(8,128)}, /*in...) custom-call(f32[768,768]{1,0:T(8,128)} %bitcast.46, ...), custom_call_target="tpu_custom_call" | custom-call | flops 16499999744 | bytes 45000000 | tf_op jit(solution)/shard_map/adam/pallas_call | solution.py:1399
  464.8 0.0 copy-start
  464.8 0.0 copy-done.2
  464.8 1.0 copy.65
  465.9 1.1 copy-done
  466.9 1.4 copy.66
  (7 shorter events, 0.1 us)
Async XLA Ops:
  3.2 2.4 copy-start.4
  3.2 3.1 copy-start.1
  443.2 3.4 copy-start.3
  448.2 16.7 %copy-start.2 = (bf16[788,768]{1,0:T(8,128)(2,1)S(1)}, bf16[788,768]{1,0:T(8,128)(2,1)}, u32[]{:S(2)}) copy-start(bf16[788,768]{1,0:T(8,128)(2,1)} %get-tuple-element.138) | copy-start | bytes 3631108
  464.8 2.1 copy-start

commit v3 on v2

--- a/solution.py
+++ b/solution.py
@@ -495,8 +495,6 @@
     recv_sem,
     w_send,
     w_recv,
-    sib_send,
-    sib_recv,
     own_sem,
     load_sem,
     *,
@@ -522,17 +520,6 @@
 
     pieces = w_send.shape[0] // 2
     piece = 2 * width // pieces
-
-    def sib_copy(k, j):
-        at = pl.ds(j * piece, piece)
-        return pltpu.make_async_remote_copy(
-            src_ref=w_ref.at[k, at],
-            dst_ref=w_ref.at[2 + k, at],
-            send_sem=sib_send.at[k * pieces + j],
-            recv_sem=sib_recv.at[k * pieces + j],
-            device_id=sibling,
-            device_id_type=MESH,
-        )
 
     w_copies = [
         [
@@ -635,7 +622,6 @@
         for j in range(pieces):
             for k in range(2):
                 w_copies[k][j][1]()
-                sib_copy(k, j).start()
         for k in sum(early, []):
             swap_copy(k).wait()
         own_copy.wait()
@@ -643,7 +629,6 @@
         for j in range(pieces):
             for k in range(2):
                 w_copies[k][j][2]()
-                sib_copy(k, j).wait()
 
 
 def expert_kernel(
@@ -671,6 +656,7 @@
     w_sem,
     own_sem,
     pair_sem,
+    sib_sem,
     ready_sem,
     *,
     experts,
@@ -709,8 +695,16 @@
         )
 
     weights = [
-        pltpu.make_async_copy(w_ref.at[j], w_all.at[j], w_sem.at[j]) for j in range(4)
-    ]
+        pltpu.make_async_remote_copy(
+            src_ref=w_ref.at[j],
+            dst_ref=w_all.at[2 + j],
+            send_sem=sib_sem.at[j],
+            recv_sem=sib_sem.at[2 + j],
+            device_id=sibling,
+            device_id_type=MESH,
+        )
+        for j in range(2)
+    ] + [pltpu.make_async_copy(w_ref.at[j], w_all.at[j], w_sem.at[j]) for j in range(2)]
     for copy in weights:
         copy.start()
     g_copy = pltpu.make_async_copy(g_ref, g_all, g_sem)
@@ -956,6 +950,8 @@
         for j in range(turns):
             aside[j].start()
         direct[0]()
+        for k in range(experts - 1, 0, -1):
+            swap_copy(k).start()
         own_copy.start()
         small[...] = wall_ref[0, :, 2 * width :].astype(F32).T
         acc[...] = jnp.zeros_like(acc)
@@ -1044,8 +1040,6 @@
         def _(j=j):
             aside[j].wait_recv()
             passed[j][0]()
-            for k in list(range(experts - 1, 0, -1))[j::turns]:
-                swap_copy(k).start()
 
     @pl.when(step == pl.num_programs(0) - 1)
     def _():
@@ -1204,7 +1198,7 @@
                 struct((images, experts, PAD), F32),
                 struct((experts, cap, width), BF16),
                 struct((2,) + block, BF16),
-                struct((4, 2 * width, slice_width), BF16),
+                struct((2, 2 * width, slice_width), BF16),
                 struct((images, PAD, width), BF16),
                 struct((images, PAD, width), BF16),
                 struct((2, tokens), jnp.int32),
@@ -1245,7 +1239,7 @@
             ]
             + [dma((2, count))] * 4
             + [dma((experts,))] * 2
-            + [dma((8,))] * 4
+            + [dma((8,))] * 2
             + [dma((2,))] * 2,
             compiler_params=params(collective_id=0, has_side_effects=True),
             cost_estimate=cost(120),
@@ -1282,7 +1276,7 @@
             pltpu.VMEM((group * cap, width), F32),
         ]
         + [dma((experts,))] * 5
-        + [dma, dma((4,)), dma, dma((4,)), pltpu.SemaphoreType.REGULAR],
+        + [dma, dma((4,)), dma, dma((4,)), dma((4,)), pltpu.SemaphoreType.REGULAR],
         compiler_params=params(collective_id=1, has_side_effects=True),
         cost_estimate=cost(140),
         name="experts",
@@ -1372,7 +1366,7 @@
         2.0 * width ** (-0.5),
         2.0 * max(1, FF * 4 // (experts * experts)) ** (-0.5),
     )
-    step_rows = 128
+    step_rows = width // 2 if width % 256 == 0 else 128
 
     def rows_spec(cols):
         return pl.BlockSpec((step_rows, cols), lambda i: (i, 0))

time: 477 us -> 461 us (0.966)
  the two profiles are of different devices: /device:TPU:7 before, /device:TPU:0 now
where the time goes in v3:
time: 461 us; the launch traced here: 453 us
  Pallas kernels  436 us (95%)
  local copies, waits for them, and re-layouts  15.8 us (3%)
    pallas_call x1, Pallas kernels, on_device(): pl.pallas_call(functools.partial(forward_kernel, experts=experts, cap=cap...  150 us
    pallas_call x1, Pallas kernels, on_device(): pl.pallas_call(functools.partial(backward_kernel, experts=experts, cap=ca...  147 us
    pallas_call x1, Pallas kernels, on_device(): pl.pallas_call(functools.partial(expert_kernel, experts=experts, cap=cap,...  124 us
    pallas_call x1, Pallas kernels, on_device(): pl.pallas_call(functools.partial(adam_kernel, rates=rates, shapes=(half_w...  15.7 us

profile of v3, /device:TPU:0, one launch (start us, length us, event | category | flops | bytes accessed | tf_op | source)
XLA Modules:
  0.0 452.7 jit_solution(9907947521618874302)
XLA Ops:
  0.7 0.8 reshape.98
  1.4 0.8 copy.57
  2.2 0.8 copy.56
  3.0 0.2 copy.58
  3.2 0.0 copy-start.4
  3.2 0.0 copy-start.1
  3.2 0.8 copy.59.wide_in
  4.0 1.2 reshape.96
  5.3 0.1 copy.55
  5.3 0.1 reshape.97
  5.5 0.0 copy-done.4
  5.5 0.8 concatenate.6.own_ref
  6.3 0.0 copy-done.1
  6.3 149.5 %forward.1 = (bf16[4,208,2304]{2,1,0:T(8,128)(2,1)}, bf16[4,208,768]{2,1,0:T(8,128)(2,1)}, f32[4,208,768]{2,1,0:T(8,128)}, bf16[4,208,768]{2,1,0:T(8,128)(2,1)},...) custom-call(bf16[788,768]{1,0:T(8,128)(2,1)} %x_ref.1, ...), custom_call_target="tpu_custom_call" | custom-call | flops 131999997952 | bytes 360000000 | tf_op jit(solution)/shard_map/forward/pallas_call | solution.py:1190
  155.9 0.9 slice_bitcast_fusion
  156.8 0.7 copy.60.router_ref
  157.6 123.9 %experts.1 = (bf16[8,320,768]{2,1,0:T(8,128)(2,1)}, bf16[8,336,768]{2,1,0:T(8,128)(2,1)}, bf16[2,1536,768]{2,1,0:T(8,128)(2,1)}) custom-call(s32[2,832]{1,0:T(2,128)} %get-tuple-element.77.wide_ref, bf16[832,768]{1,0:T(8,128)(2,1)} %bitcast.61, bf16[8,320,768]{2,1,0:T(8,128)(2,1)} %get-tuple-element.79.g_ref, bf16[2,1536,768]{2,1,0:T(8,128)(2,1)} %get-tuple-element.80.w_ref, ...), custom_call_target="tpu_custom_call" | custom-call | flops 153999998976 | bytes 420000000 | tf_op jit(solution)/shard_map/experts/pallas_call | solution.py:1260
  281.5 146.7 %backward.1 = (f32[788,768]{1,0:T(8,128)}, bf16[788,768]{1,0:T(8,128)(2,1)}, f32[24,3328]{1,0:T(8,128)}, bf16[2,1536,768]{2,1,0:T(8,128)(2,1)}, bf16[4,384,768]{2,1,0:T(8,128)(2,1)}) custom-call(s32[4,208,2]{2,1,0:T(8,128)} %get-tuple-element.69.tall_ref, bf16[4,208,768]{2,1,0:T(8,128)(2,1)} %get-tuple-element.70.gy_ref, ...), custom_call_target="tpu_custom_call" | custom-call | flops 131999997952 | bytes 360000000 | tf_op jit(solution)/shard_map/backward/pallas_call | solution.py:1296
  428.1 0.0 copy-start.3
  428.2 1.0 slice.28
  429.1 0.9 slice.27
  430.1 0.1 reshape.108
  430.2 0.2 copy.61
  430.4 1.1 reshape.109.refs_22_
  431.5 0.0 copy-done.3
  431.5 0.5 copy.62
  432.0 0.6 slice.37.refs_24_
  432.6 0.6 slice.36.refs_23_
  433.2 0.0 copy-start.2
  433.2 15.7 %adam.1 = (f32[24,2304]{1,0:T(8,128)}, f32[24,2304]{1,0:T(8,128)}, f32[24,2304]{1,0:T(8,128)}, bf16[24,2304]{1,0:T(8,128)(2,1)}, f32[24,768]{1,0:T(8,128)}, /*in...) custom-call(f32[768,768]{1,0:T(8,128)} %bitcast.46, ...), custom_call_target="tpu_custom_call" | custom-call | flops 16499999744 | bytes 45000000 | tf_op jit(solution)/shard_map/adam/pallas_call | solution.py:1393
  448.9 0.0 copy-start
  448.9 0.0 copy-done.2
  448.9 1.0 copy.65
  449.9 1.1 copy-done
  451.0 1.4 copy.66
  (7 shorter events, 0.1 us)
Async XLA Ops:
  3.2 2.4 copy-start.4
  3.2 3.1 copy-start.1
  428.1 3.4 copy-start.3
  433.2 15.7 %copy-start.2 = (bf16[788,768]{1,0:T(8,128)(2,1)S(1)}, bf16[788,768]{1,0:T(8,128)(2,1)}, u32[]{:S(2)}) copy-start(bf16[788,768]{1,0:T(8,128)(2,1)} %get-tuple-element.138) | copy-start | bytes 3631108
  448.9 2.1 copy-start
